TPU v7x, 32 devices: a whole 2x2x4 slice. The times are simulated.
32 devices in a mesh: seq: 16 (over z, x, core), batch: 2 (over y).
Axes of the slice: x: 2, y: 2, z: 4, core: 2. Of those that a mesh axis runs over, the one named last changes fastest.
Arguments:
- bases: int32 [16384, 128], P(('batch', 'seq')), parts along dimension 0, may hold values from 0 to 3
- embed_table: bfloat16 [512, 768], replicated, may hold values from -0.5 to 0.5
- norm_gains: float32 [3, 768], replicated, may hold values from 0.1 to 1.9
- depth_taps: float32 [3, 5, 768], replicated, may hold values from -2.5 to 2.5
- point_weight: bfloat16 [3, 768, 768], replicated, may hold values from -0.21875 to 0.21875
- query_weight: bfloat16 [768, 128], replicated, may hold values from -0.5390625 to 0.5390625
- key_weight: bfloat16 [768, 128], replicated, may hold values from -0.5390625 to 0.5390625
- pair_kernel: bfloat16 [3, 3, 128, 128], replicated, may hold values from -0.1875 to 0.1875
Outputs:
- trunk: bfloat16 [16384, 768], P(('batch', 'seq')), parts along dimension 0
- pair_map: bfloat16 [1024, 512, 128], P(('batch', 'seq')), parts along dimension 0
There are 2 independent parts, one for each index of `batch`. A program takes and returns all parts, laid end to end along the dimension named above; an argument that names none is the same for every part. Nothing has to cross between parts.
All inputs are finite; a program needn't handle non-finite values.
Results may differ from a plain program's by a relative error of at most 0.018.
Values may be sent and summed in bfloat16 or wider, within the bound.
A program may use at most 128 MiB of HBM per device.

v0:
```python
import jax
import jax.numpy as jnp
from jax import lax
from jax.sharding import PartitionSpec as P

KW = 5
FIRST_DILATION = 2
SECOND_DILATION = 8
THIRD_DILATION = 32
POOL = 16


def with_halo(cells, sides, width):
    for axis, dim in sides:
        count = lax.axis_size(axis)
        ends = count - 1
        head = lax.slice_in_dim(cells, 0, width, axis=dim)
        tail = lax.slice_in_dim(cells, cells.shape[dim] - width, cells.shape[dim], axis=dim)
        cells = jnp.concatenate(
            [
                lax.ppermute(tail, axis, [(i, (i + 1) % count) for i in range(ends)]),
                cells,
                lax.ppermute(head, axis, [((i + 1) % count, i) for i in range(ends)]),
            ],
            axis=dim,
        )
    return cells


def embed_bases(bases, embed_table):
    one_hot_bases = (bases[:, :, None] == jnp.arange(4, dtype=jnp.int32)).astype(jnp.bfloat16)
    one_hot_bases = one_hot_bases.reshape(bases.shape[0], -1)
    return jnp.dot(one_hot_bases, embed_table, preferred_element_type=jnp.float32).astype(
        jnp.bfloat16
    )


def normalize(value_rows, gain):
    floats = value_rows.astype(jnp.float32)
    scale = lax.rsqrt(jnp.mean(floats * floats, axis=-1, keepdims=True) + 1e-06)
    return (floats * scale * gain).astype(jnp.bfloat16)


def mix_rows(inner, normed, taps, point, dilation_reach, rows):
    summed = jnp.zeros((rows, normed.shape[1]), jnp.float32)
    for offset in range(KW):
        summed = (
            summed
            + normed[offset * dilation_reach : offset * dilation_reach + rows].astype(jnp.float32)
            * taps[offset]
        )
    activated = jax.nn.gelu(summed).astype(jnp.bfloat16)
    return (
        inner.astype(jnp.float32) + jnp.dot(activated, point, preferred_element_type=jnp.float32)
    ).astype(jnp.bfloat16)


def pair_conv(extended, pair_kernel, rows, width):
    padded = jnp.pad(extended, ((0, 0), (1, 1), (0, 0)))
    channels = extended.shape[2]
    summed = jnp.zeros((rows * width, channels), jnp.float32)
    for row_tap in range(3):
        for col_tap in range(3):
            window = padded[row_tap : row_tap + rows, col_tap : col_tap + width].reshape(
                rows * width, channels
            )
            summed = summed + jnp.dot(
                window, pair_kernel[row_tap, col_tap], preferred_element_type=jnp.float32
            )
    center = extended[1 : rows + 1].astype(jnp.float32).reshape(rows * width, channels)
    return (center + jax.nn.gelu(summed)).astype(jnp.bfloat16).reshape(rows, width, channels)


def on_device(
    bases, embed_table, norm_gains, depth_taps, point_weight, query_weight, key_weight, pair_kernel
):
    dilation_reaches = (FIRST_DILATION, SECOND_DILATION, THIRD_DILATION)
    current = embed_bases(bases, embed_table)
    slab_rows = current.shape[0]
    for trunk_layer in range(3):
        dilation_reach = dilation_reaches[trunk_layer]
        normed = normalize(current, norm_gains[trunk_layer])
        widened = with_halo(normed, (("seq", 0),), 2 * dilation_reach)
        current = mix_rows(
            current,
            widened,
            depth_taps[trunk_layer],
            point_weight[trunk_layer],
            dilation_reach,
            slab_rows,
        )
    pooled = jnp.mean(
        current.astype(jnp.float32).reshape(-1, POOL, current.shape[1]), axis=1
    ).astype(jnp.bfloat16)
    queries = jnp.dot(pooled, query_weight, preferred_element_type=jnp.float32).astype(jnp.bfloat16)
    all_keys = jnp.dot(
        lax.all_gather(pooled, "seq", axis=0, tiled=True),
        key_weight,
        preferred_element_type=jnp.float32,
    ).astype(jnp.bfloat16)
    key_floats = all_keys.astype(jnp.float32)[None, :, :]
    pair_rows = queries.shape[0]
    pair = (queries.astype(jnp.float32)[:, None, :] * key_floats).astype(jnp.bfloat16)
    extended = with_halo(pair, (("seq", 0),), 1)
    pair_map = pair_conv(extended, pair_kernel, pair_rows, all_keys.shape[0])
    return (current, pair_map)


def solution(mesh):
    return jax.shard_map(
        on_device,
        mesh=mesh,
        in_specs=(P(("batch", "seq"), None), P(), P(), P(), P(), P(), P(), P()),
        out_specs=(P(("batch", "seq"), None), P(("batch", "seq"), None, None)),
        check_vma=False,
    )
```

profile of v0, /device:TPU:1, one launch (start us, length us, event | category | flops | bytes accessed | tf_op | source)
XLA Modules:
  0.0 121.6 jit_solution(9066388841470635529)
XLA Ops:
  0.6 0.0 copy-start
  0.6 1.1 copy.10
  1.8 0.0 copy-start.13
  1.8 0.2 eq.20
  2.0 0.4 eq.21
  2.4 0.1 eq.23
  2.5 0.0 copy-done.13
  2.5 0.0 copy-done
  2.6 0.0 copy-start.12
  2.6 0.0 copy-start.14
  2.6 0.9 fusion.16
  3.5 0.3 fusion.18
  3.7 4.5 %collective-permute-start = (bf16[4,768]{1,0:T(4,128)(2,1)S(1)}, bf16[4,768]{1,0:T(4,128)(2,1)S(1)}, u32[]{:S(2)}, u32[]{:S(2)}) collective-permute-start(bf16[4,768]{1,0:T(4,128)(2,1)S(1)} %get-tuple-element.34), channel_id=1, source_target_pairs={{0,2},{2,4},{4,6},{6,8},{8,10},{10,12},{12,14},{14,16},{16,18},{18... | collective-permute-start | bytes 18440 | tf_op jit(solution)/shard_map/ppermute | solution.py:21
  8.3 1.9 %collective-permute-start.1 = (bf16[4,768]{1,0:T(4,128)(2,1)S(1)}, bf16[4,768]{1,0:T(4,128)(2,1)S(1)}, u32[]{:S(2)}, u32[]{:S(2)}) collective-permute-start(bf16[4,768]{1,0:T(4,128)(2,1)S(1)} %get-tuple-element.35), channel_id=1, source_target_pairs={{2,0},{4,2},{6,4},{8,6},{10,8},{12,10},{14,12},{16,14},{18,16},{20... | collective-permute-start | bytes 18440 | tf_op jit(solution)/shard_map/ppermute | solution.py:23
  10.2 0.0 copy-done.12
  10.2 0.1 slice_reduce_fusion.4
  10.3 0.0 collective-permute-done
  10.3 2.9 %collective-permute-done.1 = bf16[4,768]{1,0:T(4,128)(2,1)S(1)} collective-permute-done((bf16[4,768]{1,0:T(4,128)(2,1)S(1)}, bf16[4,768]{1,0:T(4,128)(2,1)S(1)}, u32[]{:S(2)}, u32[]{:S(2)}) %collective-permute-start.1) | collective-permute-done | bytes 6176 | tf_op jit(solution)/shard_map/ppermute | solution.py:23
  13.2 0.0 copy-done.14
  13.2 2.1 %fusion.28 = (f32[512]{0:T(512)S(1)}, bf16[512,768]{1,0:T(8,128)(2,1)S(1)}) fusion(bf16[3,768,768]{2,1,0:T(8,128)(2,1)S(1)} %copy-done.14, bf16[512,768]{1,0:T(8,128)(2,1)S(1)} %fusion.18, bf16[4,768]{1,0:T(4,128)(2,1)S(1)} %collective-permute-done.1, bf16[4,768]{1,0:T(4,128)(2,1)S(1)} %collective-permute-done, f32[768]{0:T(1024)S(1)} %get-tuple-element.10, ...), kind=kOutput, calls=%fused_computation.53 | convolution fusion | flops 620101120 | bytes 3573760 | tf_op jit(solution)/shard_map/dot_general | solution.py:54
  15.3 0.3 fusion.30
  15.6 1.9 %collective-permute-start.2 = (bf16[16,768]{1,0:T(8,128)(2,1)S(1)}, bf16[16,768]{1,0:T(8,128)(2,1)S(1)}, u32[]{:S(2)}, u32[]{:S(2)}) collective-permute-start(bf16[16,768]{1,0:T(8,128)(2,1)S(1)} %get-tuple-element.32), channel_id=1, source_target_pairs={{0,2},{2,4},{4,6},{6,8},{8,10},{10,12},{12,14},{14,16},{16,18},{18... | collective-permute-start | bytes 73736 | tf_op jit(solution)/shard_map/ppermute | solution.py:21
  17.5 2.4 %collective-permute-start.3 = (bf16[16,768]{1,0:T(8,128)(2,1)S(1)}, bf16[16,768]{1,0:T(8,128)(2,1)S(1)}, u32[]{:S(2)}, u32[]{:S(2)}) collective-permute-start(bf16[16,768]{1,0:T(8,128)(2,1)S(1)} %get-tuple-element.33), channel_id=1, source_target_pairs={{2,0},{4,2},{6,4},{8,6},{10,8},{12,10},{14,12},{16,14},{18,16},{20... | collective-permute-start | bytes 73736 | tf_op jit(solution)/shard_map/ppermute | solution.py:23
  19.9 0.0 collective-permute-done.2
  19.9 3.5 %collective-permute-done.3 = bf16[16,768]{1,0:T(8,128)(2,1)S(1)} collective-permute-done((bf16[16,768]{1,0:T(8,128)(2,1)S(1)}, bf16[16,768]{1,0:T(8,128)(2,1)S(1)}, u32[]{:S(2)}, u32[]{:S(2)}) %collective-permute-start.3) | collective-permute-done | bytes 24608 | tf_op jit(solution)/shard_map/ppermute | solution.py:23
  23.5 1.7 %fusion.40 = (f32[512]{0:T(512)S(1)}, bf16[512,768]{1,0:T(8,128)(2,1)S(1)}) fusion(bf16[3,768,768]{2,1,0:T(8,128)(2,1)S(1)} %copy-done.14, bf16[512,768]{1,0:T(8,128)(2,1)S(1)} %fusion.30, bf16[16,768]{1,0:T(8,128)(2,1)S(1)} %collective-permute-done.3, bf16[16,768]{1,0:T(8,128)(2,1)S(1)} %collective-permute-done.2, f32[768]{0:T(1024)S(1)} %get-tuple-element.5, ...), kind=kOutput, calls=%fused_computation.65 | convolution fusion | flops 620101120 | bytes 3610624 | tf_op jit(solution)/shard_map/dot_general | solution.py:54
  25.2 0.3 fusion.42
  25.5 1.9 %collective-permute-start.4 = (bf16[64,768]{1,0:T(8,128)(2,1)S(1)}, bf16[64,768]{1,0:T(8,128)(2,1)S(1)}, u32[]{:S(2)}, u32[]{:S(2)}) collective-permute-start(bf16[64,768]{1,0:T(8,128)(2,1)S(1)} %get-tuple-element.30), channel_id=1, source_target_pairs={{0,2},{2,4},{4,6},{6,8},{8,10},{10,12},{12,14},{14,16},{16,18},{18... | collective-permute-start | bytes 294920 | tf_op jit(solution)/shard_map/ppermute | solution.py:21
  27.4 2.4 %collective-permute-start.5 = (bf16[64,768]{1,0:T(8,128)(2,1)S(1)}, bf16[64,768]{1,0:T(8,128)(2,1)S(1)}, u32[]{:S(2)}, u32[]{:S(2)}) collective-permute-start(bf16[64,768]{1,0:T(8,128)(2,1)S(1)} %get-tuple-element.31), channel_id=1, source_target_pairs={{2,0},{4,2},{6,4},{8,6},{10,8},{12,10},{14,12},{16,14},{18,16},{20... | collective-permute-start | bytes 294920 | tf_op jit(solution)/shard_map/ppermute | solution.py:23
  29.9 0.0 collective-permute-done.4
  29.9 4.4 %collective-permute-done.5 = bf16[64,768]{1,0:T(8,128)(2,1)S(1)} collective-permute-done((bf16[64,768]{1,0:T(8,128)(2,1)S(1)}, bf16[64,768]{1,0:T(8,128)(2,1)S(1)}, u32[]{:S(2)}, u32[]{:S(2)}) %collective-permute-start.5) | collective-permute-done | bytes 98336 | tf_op jit(solution)/shard_map/ppermute | solution.py:23
  34.3 3.7 %convert_reduce_fusion = (f32[32,768]{1,0:T(8,128)S(1)}, bf16[512,768]{1,0:T(8,128)(2,1)}) fusion(bf16[3,768,768]{2,1,0:T(8,128)(2,1)S(1)} %copy-done.14, bf16[512,768]{1,0:T(8,128)(2,1)S(1)} %fusion.42, bf16[64,768]{1,0:T(8,128)(2,1)S(1)} %collective-permute-done.5, bf16[64,768]{1,0:T(8,128)(2,1)S(1)} %collective-permute-done.4, ...), kind=kOutput, calls=%fused_computation.77 | convolution fusion | flops 619683840 | bytes 3854336 | tf_op jit(solution)/shard_map/dot_general | solution.py:54
  38.0 21.5 %all_gather.3 = bf16[512,768]{1,0:T(8,128)(2,1)S(1)} all-gather(bf16[32,768]{1,0:T(8,128)(2,1)S(1)} %multiply_convert_fusion.1), channel_id=1, replica_groups=mesh['seq'=16,'batch'=2] {'seq'}, dimensions={0}, use_global_device_ids=true | all-gather | bytes 835584 | tf_op jit(solution)/shard_map/all_gather | solution.py:97
  59.5 0.0 copy-done.11
  59.5 0.1 fusion.59
  59.7 0.0 copy-done.10
  59.7 0.4 fusion.58
  60.1 1.1 multiply_convert_fusion
  61.2 0.0 copy-start.2
  61.2 1.9 %collective-permute-start.6 = (bf16[1,512,128]{2,1,0:T(8,128)(2,1)S(1)}, bf16[1,512,128]{2,1,0:T(8,128)(2,1)S(1)}, u32[]{:S(2)}, u32[]{:S(2)}) collective-permute-start(bf16[1,512,128]{2,1,0:T(8,128)(2,1)S(1)} %get-tuple-element.28), channel_id=1, source_target_pairs={{0,2},{2,4},{4,6},{6,8},{8,10},{10,12},{12,14},{14,16},{16,18},{18... | collective-permute-start | bytes 393224 | tf_op jit(solution)/shard_map/ppermute | solution.py:21
  63.1 2.6 %collective-permute-start.7 = (bf16[1,512,128]{2,1,0:T(8,128)(2,1)S(1)}, bf16[1,512,128]{2,1,0:T(8,128)(2,1)S(1)}, u32[]{:S(2)}, u32[]{:S(2)}) collective-permute-start(bf16[1,512,128]{2,1,0:T(8,128)(2,1)S(1)} %get-tuple-element.29), channel_id=1, source_target_pairs={{2,0},{4,2},{6,4},{8,6},{10,8},{12,10},{14,12},{16,14},{18,16},{20... | collective-permute-start | bytes 393224 | tf_op jit(solution)/shard_map/ppermute | solution.py:23
  65.7 0.0 collective-permute-done.6
  65.7 3.7 %collective-permute-done.7 = bf16[1,512,128]{2,1,0:T(8,128)(2,1)S(1)} collective-permute-done((bf16[1,512,128]{2,1,0:T(8,128)(2,1)S(1)}, bf16[1,512,128]{2,1,0:T(8,128)(2,1)S(1)}, u32[]{:S(2)}, u32[]{:S(2)}) %collective-permute-start.7) | collective-permute-done | bytes 131104 | tf_op jit(solution)/shard_map/ppermute | solution.py:23
  69.4 0.0 copy-done.2
  69.4 4.6 %fusion.15 = bf16[34,514,128]{2,1,0:T(8,128)(2,1)} fusion(bf16[1,512,128]{2,1,0:T(8,128)(2,1)S(1)} %collective-permute-done.7, bf16[32,512,128]{2,1,0:T(8,128)(2,1)S(1)} %multiply_convert_fusion, bf16[1,512,128]{2,1,0:T(8,128)(2,1)S(1)} %collective-permute-done.6), kind=kLoop, calls=%fused_computation.26 | loop fusion | flops 26843136 | bytes 8930304 | tf_op jit(solution)/shard_map/concatenate | solution.py:19
  74.1 17.2 %fusion.106 = (bf16[32,512,128]{2,1,0:T(8,128)(2,1)}, bf16[32,512,128]{2,1,0:T(8,128)(2,1)}, bf16[32,512,128]{2,1,0:T(8,128)(2,1)}, bf16[32,512,128]{2,1,0:T(8,1...) fusion(bf16[34,514,128]{2,1,0:T(8,128)(2,1)} %fusion.15), kind=kLoop, calls=%fused_computation.172 | loop fusion | bytes 50331648 | tf_op jit(solution)/shard_map/slice | solution.py:64
  91.2 0.0 copy-done.9
  91.2 0.0 copy-start.8
  91.2 3.6 %fusion.80 = f32[16384,128]{1,0:T(8,128)S(1)} fusion(bf16[16384,128]{1,0:T(8,128)(2,1)} %bitcast.79, bf16[3,3,128,128]{3,2,1,0:T(8,128)(2,1)S(1)} %copy-done.9), kind=kOutput, calls=%fused_computation.125 | convolution fusion | flops 536870912 | bytes 12615680 | tf_op jit(solution)/shard_map/dot_general | solution.py:67
  94.8 4.5 %fusion.71 = f32[16384,128]{1,0:T(8,128)} fusion(bf16[16384,128]{1,0:T(8,128)(2,1)S(1)} %bitcast.78, bf16[3,3,128,128]{3,2,1,0:T(8,128)(2,1)S(1)} %copy-done.9), kind=kOutput, calls=%fused_computation.116 | convolution fusion | flops 536870912 | bytes 12615680 | tf_op jit(solution)/shard_map/dot_general | solution.py:67
  99.3 2.4 %pad_maximum_fusion = (bf16[32,512,128]{2,1,0:T(8,128)(2,1)}, bf16[32,512,128]{2,1,0:T(8,128)(2,1)S(1)}) fusion(bf16[1,512,128]{2,1,0:T(8,128)(2,1)S(1)} %collective-permute-done.7, bf16[32,512,128]{2,1,0:T(8,128)(2,1)S(1)} %copy-done.3, bf16[1,512,128]{2,1,0:T(8,128)(2,1)S(1)} %collective-permute-done.6), kind=kLoop, calls=%fused_computation.27 | loop fusion | flops 4194304 | bytes 12845056 | tf_op jit(solution)/shard_map/concatenate | solution.py:19
  101.7 1.2 %convolution_add_fusion.6 = f32[16384,128]{1,0:T(8,128)S(1)} fusion(f32[16384,128]{1,0:T(8,128)S(1)} %fusion.80, bf16[16384,128]{1,0:T(8,128)(2,1)S(1)} %bitcast.77, bf16[3,3,128,128]{3,2,1,0:T(8,128)(2,1)S(1)} %copy-done.9), kind=kOutput, calls=%fused_computation.7 | convolution fusion | flops 538968064 | bytes 21004288 | tf_op jit(solution)/shard_map/dot_general | solution.py:67
  102.9 0.9 copy-done.7
  103.8 1.2 %convolution_add_fusion.5 = f32[16384,128]{1,0:T(8,128)S(1)} fusion(f32[16384,128]{1,0:T(8,128)S(1)} %convolution_add_fusion.6, bf16[16384,128]{1,0:T(8,128)(2,1)S(1)} %bitcast.76, bf16[3,3,128,128]{3,2,1,0:T(8,128)(2,1)S(1)} %copy-done.9), kind=kOutput, calls=%fused_computation.6 | convolution fusion | flops 538968064 | bytes 21004288 | tf_op jit(solution)/shard_map/dot_general | solution.py:67
  105.1 0.9 copy-done.6
  106.0 1.2 %convolution_add_fusion.4 = f32[16384,128]{1,0:T(8,128)S(1)} fusion(f32[16384,128]{1,0:T(8,128)S(1)} %convolution_add_fusion.5, bf16[16384,128]{1,0:T(8,128)(2,1)S(1)} %bitcast.75, bf16[3,3,128,128]{3,2,1,0:T(8,128)(2,1)S(1)} %copy-done.9), kind=kOutput, calls=%fused_computation.5 | convolution fusion | flops 538968064 | bytes 21004288 | tf_op jit(solution)/shard_map/dot_general | solution.py:67
  107.3 1.2 %convolution_add_fusion.3 = f32[16384,128]{1,0:T(8,128)S(1)} fusion(f32[16384,128]{1,0:T(8,128)S(1)} %convolution_add_fusion.4, bf16[16384,128]{1,0:T(8,128)(2,1)S(1)} %bitcast.71, bf16[3,3,128,128]{3,2,1,0:T(8,128)(2,1)S(1)} %copy-done.9), kind=kOutput, calls=%fused_computation.4 | convolution fusion | flops 538968064 | bytes 21004288 | tf_op jit(solution)/shard_map/dot_general | solution.py:67
  108.5 0.9 copy-done.5
  109.5 1.2 %convolution_add_fusion.2 = f32[16384,128]{1,0:T(8,128)S(1)} fusion(f32[16384,128]{1,0:T(8,128)S(1)} %convolution_add_fusion.3, bf16[16384,128]{1,0:T(8,128)(2,1)S(1)} %bitcast.74, bf16[3,3,128,128]{3,2,1,0:T(8,128)(2,1)S(1)} %copy-done.9), kind=kOutput, calls=%fused_computation.3 | convolution fusion | flops 538968064 | bytes 21004288 | tf_op jit(solution)/shard_map/dot_general | solution.py:67
  110.7 0.9 copy-done.4
  111.6 1.2 %convolution_add_fusion.1 = f32[16384,128]{1,0:T(8,128)S(1)} fusion(f32[16384,128]{1,0:T(8,128)S(1)} %convolution_add_fusion.2, bf16[16384,128]{1,0:T(8,128)(2,1)S(1)} %bitcast.73, bf16[3,3,128,128]{3,2,1,0:T(8,128)(2,1)S(1)} %copy-done.9), kind=kOutput, calls=%fused_computation.2 | convolution fusion | flops 538968064 | bytes 21004288 | tf_op jit(solution)/shard_map/dot_general | solution.py:67
  112.9 0.0 slice-done
  112.9 1.4 %slice-done.1 = s8[4194304]{0:T(1024)(128)(4,1)S(1)} async-done(((s8[8388608]{0:T(1024)(128)(4,1)}), s8[4194304]{0:T(1024)(128)(4,1)S(1)}, s32[]{:S(2)}) %slice-start.1) | async-done | bytes 4194328
  114.3 7.3 %fusion.10 = bf16[16384,128]{1,0:T(8,128)(2,1)} fusion(f32[16384,128]{1,0:T(8,128)S(1)} %bitcast.81, f32[16384,128]{1,0:T(8,128)S(1)} %convolution_add_fusion.1, bf16[16384,128]{1,0:T(8,128)(2,1)} %bitcast.82, bf16[16384,128]{1,0:T(8,128)(2,1)S(1)} %bitcast.72, bf16[3,3,128,128]{3,2,1,0:T(8,128)(2,1)S(1)} %copy-done.9), kind=kOutput, calls=%fused_computation.20 | convolution fusion | flops 564133888 | bytes 29392896 | tf_op jit(solution)/shard_map/dot_general | solution.py:67
  (25 shorter events, 0.1 us)
Async XLA Ops:
  0.6 1.9 %copy-start = (bf16[512,768]{1,0:T(8,128)(2,1)S(1)}, bf16[512,768]{1,0:T(8,128)(2,1)}, u32[]{:S(2)}) copy-start(bf16[512,768]{1,0:T(8,128)(2,1)} %param.9) | copy-start | bytes 2359300
  1.8 0.7 copy-start.13
  2.6 7.6 %copy-start.12 = (f32[3,5,768]{2,0,1:T(4,128)S(1)}, f32[3,5,768]{2,0,1:T(4,128)}, u32[]{:S(2)}) copy-start(f32[3,5,768]{2,0,1:T(4,128)} %param.11) | copy-start | bytes 138244
  2.6 10.6 %copy-start.14 = (bf16[3,768,768]{2,1,0:T(8,128)(2,1)S(1)}, bf16[3,768,768]{2,1,0:T(8,128)(2,1)}, u32[]{:S(2)}) copy-start(bf16[3,768,768]{2,1,0:T(8,128)(2,1)} %param.12) | copy-start | bytes 10616836
  3.7 6.6 %collective-permute-start = (bf16[4,768]{1,0:T(4,128)(2,1)S(1)}, bf16[4,768]{1,0:T(4,128)(2,1)S(1)}, u32[]{:S(2)}, u32[]{:S(2)}) collective-permute-start(bf16[4,768]{1,0:T(4,128)(2,1)S(1)} %get-tuple-element.34), channel_id=1, source_target_pairs={{0,2},{2,4},{4,6},{6,8},{8,10},{10,12},{12,14},{14,16},{16,18},{18... | collective-permute-start | bytes 18440 | tf_op jit(solution)/shard_map/ppermute | solution.py:21
  8.3 4.9 %collective-permute-start.1 = (bf16[4,768]{1,0:T(4,128)(2,1)S(1)}, bf16[4,768]{1,0:T(4,128)(2,1)S(1)}, u32[]{:S(2)}, u32[]{:S(2)}) collective-permute-start(bf16[4,768]{1,0:T(4,128)(2,1)S(1)} %get-tuple-element.35), channel_id=1, source_target_pairs={{2,0},{4,2},{6,4},{8,6},{10,8},{12,10},{14,12},{16,14},{18,16},{20... | collective-permute-start | bytes 18440 | tf_op jit(solution)/shard_map/ppermute | solution.py:23
  15.6 4.3 %collective-permute-start.2 = (bf16[16,768]{1,0:T(8,128)(2,1)S(1)}, bf16[16,768]{1,0:T(8,128)(2,1)S(1)}, u32[]{:S(2)}, u32[]{:S(2)}) collective-permute-start(bf16[16,768]{1,0:T(8,128)(2,1)S(1)} %get-tuple-element.32), channel_id=1, source_target_pairs={{0,2},{2,4},{4,6},{6,8},{8,10},{10,12},{12,14},{14,16},{16,18},{18... | collective-permute-start | bytes 73736 | tf_op jit(solution)/shard_map/ppermute | solution.py:21
  17.5 5.9 %collective-permute-start.3 = (bf16[16,768]{1,0:T(8,128)(2,1)S(1)}, bf16[16,768]{1,0:T(8,128)(2,1)S(1)}, u32[]{:S(2)}, u32[]{:S(2)}) collective-permute-start(bf16[16,768]{1,0:T(8,128)(2,1)S(1)} %get-tuple-element.33), channel_id=1, source_target_pairs={{2,0},{4,2},{6,4},{8,6},{10,8},{12,10},{14,12},{16,14},{18,16},{20... | collective-permute-start | bytes 73736 | tf_op jit(solution)/shard_map/ppermute | solution.py:23
  25.5 4.3 %collective-permute-start.4 = (bf16[64,768]{1,0:T(8,128)(2,1)S(1)}, bf16[64,768]{1,0:T(8,128)(2,1)S(1)}, u32[]{:S(2)}, u32[]{:S(2)}) collective-permute-start(bf16[64,768]{1,0:T(8,128)(2,1)S(1)} %get-tuple-element.30), channel_id=1, source_target_pairs={{0,2},{2,4},{4,6},{6,8},{8,10},{10,12},{12,14},{14,16},{16,18},{18... | collective-permute-start | bytes 294920 | tf_op jit(solution)/shard_map/ppermute | solution.py:21
  27.4 6.9 %collective-permute-start.5 = (bf16[64,768]{1,0:T(8,128)(2,1)S(1)}, bf16[64,768]{1,0:T(8,128)(2,1)S(1)}, u32[]{:S(2)}, u32[]{:S(2)}) collective-permute-start(bf16[64,768]{1,0:T(8,128)(2,1)S(1)} %get-tuple-element.31), channel_id=1, source_target_pairs={{2,0},{4,2},{6,4},{8,6},{10,8},{12,10},{14,12},{16,14},{18,16},{20... | collective-permute-start | bytes 294920 | tf_op jit(solution)/shard_map/ppermute | solution.py:23
  34.3 25.2 %copy-start.11 = (bf16[768,128]{1,0:T(8,128)(2,1)S(1)}, bf16[768,128]{1,0:T(8,128)(2,1)}, u32[]{:S(2)}) copy-start(bf16[768,128]{1,0:T(8,128)(2,1)} %param.13) | copy-start | bytes 589828
  34.3 25.4 %copy-start.10 = (bf16[768,128]{1,0:T(8,128)(2,1)S(1)}, bf16[768,128]{1,0:T(8,128)(2,1)}, u32[]{:S(2)}) copy-start(bf16[768,128]{1,0:T(8,128)(2,1)} %param.14) | copy-start | bytes 589828
  61.2 8.3 %copy-start.2 = (bf16[32,512,128]{2,1,0:T(8,128)(2,1)}, bf16[32,512,128]{2,1,0:T(8,128)(2,1)S(1)}, u32[]{:S(2)}) copy-start(bf16[32,512,128]{2,1,0:T(8,128)(2,1)S(1)} %multiply_convert_fusion) | copy-start | bytes 12582916
  61.2 4.5 %collective-permute-start.6 = (bf16[1,512,128]{2,1,0:T(8,128)(2,1)S(1)}, bf16[1,512,128]{2,1,0:T(8,128)(2,1)S(1)}, u32[]{:S(2)}, u32[]{:S(2)}) collective-permute-start(bf16[1,512,128]{2,1,0:T(8,128)(2,1)S(1)} %get-tuple-element.28), channel_id=1, source_target_pairs={{0,2},{2,4},{4,6},{6,8},{8,10},{10,12},{12,14},{14,16},{16,18},{18... | collective-permute-start | bytes 393224 | tf_op jit(solution)/shard_map/ppermute | solution.py:21
  63.1 6.3 %collective-permute-start.7 = (bf16[1,512,128]{2,1,0:T(8,128)(2,1)S(1)}, bf16[1,512,128]{2,1,0:T(8,128)(2,1)S(1)}, u32[]{:S(2)}, u32[]{:S(2)}) collective-permute-start(bf16[1,512,128]{2,1,0:T(8,128)(2,1)S(1)} %get-tuple-element.29), channel_id=1, source_target_pairs={{2,0},{4,2},{6,4},{8,6},{10,8},{12,10},{14,12},{16,14},{18,16},{20... | collective-permute-start | bytes 393224 | tf_op jit(solution)/shard_map/ppermute | solution.py:23
  74.1 17.2 %copy-start.9 = (bf16[3,3,128,128]{3,2,1,0:T(8,128)(2,1)S(1)}, bf16[3,3,128,128]{3,2,1,0:T(8,128)(2,1)}, u32[]{:S(2)}) copy-start(bf16[3,3,128,128]{3,2,1,0:T(8,128)(2,1)} %param.15) | copy-start | bytes 884740
  91.2 3.6 %copy-start.8 = (bf16[32,512,128]{2,1,0:T(8,128)(2,1)S(1)}, bf16[32,512,128]{2,1,0:T(8,128)(2,1)}, u32[]{:S(2)}) copy-start(bf16[32,512,128]{2,1,0:T(8,128)(2,1)} %get-tuple-element.25) | copy-start | bytes 12582916
  94.8 4.5 %copy-start.3 = (bf16[32,512,128]{2,1,0:T(8,128)(2,1)S(1)}, bf16[32,512,128]{2,1,0:T(8,128)(2,1)}, u32[]{:S(2)}) copy-start(bf16[32,512,128]{2,1,0:T(8,128)(2,1)} %copy-done.2) | copy-start | bytes 12582916
  101.7 2.2 %copy-start.7 = (bf16[32,512,128]{2,1,0:T(8,128)(2,1)S(1)}, bf16[32,512,128]{2,1,0:T(8,128)(2,1)}, u32[]{:S(2)}) copy-start(bf16[32,512,128]{2,1,0:T(8,128)(2,1)} %get-tuple-element.23) | copy-start | bytes 12582916
  103.8 2.2 %copy-start.6 = (bf16[32,512,128]{2,1,0:T(8,128)(2,1)S(1)}, bf16[32,512,128]{2,1,0:T(8,128)(2,1)}, u32[]{:S(2)}) copy-start(bf16[32,512,128]{2,1,0:T(8,128)(2,1)} %get-tuple-element.22) | copy-start | bytes 12582916
  107.3 2.2 %copy-start.5 = (bf16[32,512,128]{2,1,0:T(8,128)(2,1)S(1)}, bf16[32,512,128]{2,1,0:T(8,128)(2,1)}, u32[]{:S(2)}) copy-start(bf16[32,512,128]{2,1,0:T(8,128)(2,1)} %get-tuple-element.21) | copy-start | bytes 12582916
  109.5 2.2 %copy-start.4 = (bf16[32,512,128]{2,1,0:T(8,128)(2,1)S(1)}, bf16[32,512,128]{2,1,0:T(8,128)(2,1)}, u32[]{:S(2)}) copy-start(bf16[32,512,128]{2,1,0:T(8,128)(2,1)} %get-tuple-element.20) | copy-start | bytes 12582916
  109.5 3.5 %slice-start = ((s8[8388608]{0:T(1024)(128)(4,1)}), s8[4194304]{0:T(1024)(128)(4,1)S(1)}, s32[]{:S(2)}) async-start(s8[8388608]{0:T(1024)(128)(4,1)} %bitcast.80), calls=%async_computation | async-start | bytes 8388608
  111.6 2.7 %slice-start.1 = ((s8[8388608]{0:T(1024)(128)(4,1)}), s8[4194304]{0:T(1024)(128)(4,1)S(1)}, s32[]{:S(2)}) async-start(s8[8388608]{0:T(1024)(128)(4,1)} %bitcast.80), calls=%async_computation.1 | async-start | bytes 8388608
  114.3 7.3 %copy-start.1 = (bf16[512,768]{1,0:T(8,128)(2,1)S(1)}, bf16[512,768]{1,0:T(8,128)(2,1)}, u32[]{:S(2)}) copy-start(bf16[512,768]{1,0:T(8,128)(2,1)} %param.9) | copy-start | bytes 2359300
where the time goes:
time: 122 us
  matrix products  31.6 us (26%)
  local copies, waits for them, and re-layouts  24.5 us (20%)
  blocking collectives  21.5 us (18%)
  starting transfers between devices  19.6 us (16%)
  waiting for transfers between devices  14.5 us (12%)
  other arithmetic  8.89 us (7%)
    dot_general x9, matrix products, pair_conv(): jnp.dot(window, pair_kernel[row_tap, col_tap], preferred_element_type=jnp...  22.7 us
    all_gather x1, blocking collectives, on_device(): lax.all_gather(pooled, 'seq', axis=0, tiled=True)  21.5 us
    slice x1, local copies, waits for them, and re-layouts, pair_conv(): padded[row_tap:row_tap + rows, col_tap:col_tap + width]  17.2 us
    ppermute x4, waiting for transfers between devices, with_halo(): lax.ppermute(head, axis, [((i + 1) % count, i) for i in range(ends)])  14.5 us
    ppermute x4, starting transfers between devices, with_halo(): lax.ppermute(tail, axis, [(i, (i + 1) % count) for i in range(ends)])  10.3 us
    ppermute x4, starting transfers between devices, with_halo(): lax.ppermute(head, axis, [((i + 1) % count, i) for i in range(ends)])  9.29 us
    dot_general x3, matrix products, mix_rows(): jnp.dot(activated, point, preferred_element_type=jnp.float32)  7.55 us
    concatenate x2, other arithmetic, with_halo(): jnp.concatenate([lax.ppermute(tail, axis, [(i, (i + 1) % count) for i in...  6.99 us
  transfers between devices with their start and end apart: 8, of which 4 were waited for; matrix products, arithmetic and copies ran while one was open for 0% of the time, Pallas kernels for 0%

commit v1 on v0

v1 whole, which is shorter than its diff:
```python
import functools

import jax
import jax.numpy as jnp
from jax import lax
from jax.experimental import pallas as pl
from jax.experimental.pallas import tpu as pltpu
from jax.sharding import PartitionSpec as P

KW = 5
DILATIONS = (2, 8, 32)
POOL = 16
HALO = 96
CHUNK = 32
GELU_A = 0.7978845608028654
GELU_B = 0.7978845608028654 * 0.044715
MESH = pl.DeviceIdType.MESH
F32 = jnp.float32
BF16 = jnp.bfloat16


def gelu(v):
    half = 0.5 * v
    return half + half * jnp.tanh(v * (GELU_A + GELU_B * (v * v)))


def trunk_kernel(
    n,
    bases,
    table,
    gains,
    taps,
    point,
    query_w,
    key_w,
    trunk_out,
    kq,
    base_v,
    table_v,
    gains_v,
    taps_v,
    point_v,
    qw_v,
    kw_v,
    hot,
    xs,
    nrm,
    act,
    trunk_v,
    local_sem,
    halo_send,
    halo_recv,
    send_sem,
    recv_sem,
):
    slab = bases.shape[0]
    channels = table.shape[1]
    full = slab + 2 * HALO
    pool_rows = slab // POOL
    me = lax.axis_index("seq")
    right = lax.rem(me + 1, n)
    left = lax.rem(me + n - 1, n)

    barrier = pltpu.get_barrier_semaphore()
    for d in range(1, n):
        pl.semaphore_signal(
            barrier, inc=1, device_id={"seq": lax.rem(me + d, n)}, device_id_type=MESH
        )

    own = pltpu.make_async_copy(bases, base_v.at[pl.ds(HALO, slab)], local_sem.at[0])
    own.start()
    get_table = pltpu.make_async_copy(table, table_v, local_sem.at[1])
    get_table.start()
    get_gains = pltpu.make_async_copy(gains, gains_v, local_sem.at[2])
    get_gains.start()
    get_taps = pltpu.make_async_copy(taps, taps_v, local_sem.at[3])
    get_taps.start()
    get_point = []
    for layer in range(3):
        get_point.append(
            pltpu.make_async_copy(point.at[layer], point_v.at[layer], local_sem.at[4 + layer])
        )
        get_point[-1].start()
    get_qw = pltpu.make_async_copy(query_w, qw_v, local_sem.at[7])
    get_qw.start()
    get_kw = pltpu.make_async_copy(key_w, kw_v, local_sem.at[8])
    get_kw.start()

    pl.semaphore_wait(barrier, n - 1)
    to_right = pltpu.make_async_remote_copy(
        src_ref=bases.at[pl.ds(slab - HALO, HALO)],
        dst_ref=base_v.at[pl.ds(0, HALO)],
        send_sem=halo_send.at[0],
        recv_sem=halo_recv.at[0],
        device_id={"seq": right},
        device_id_type=MESH,
    )
    to_right.start()
    to_left = pltpu.make_async_remote_copy(
        src_ref=bases.at[pl.ds(0, HALO)],
        dst_ref=base_v.at[pl.ds(HALO + slab, HALO)],
        send_sem=halo_send.at[1],
        recv_sem=halo_recv.at[1],
        device_id={"seq": left},
        device_id_type=MESH,
    )
    to_left.start()

    width = table.shape[0]
    places = width // 4
    spread = (
        lax.broadcasted_iota(jnp.int32, (places, width), 1) // 4
        == lax.broadcasted_iota(jnp.int32, (places, width), 0)
    ).astype(BF16)

    def embed(start, rows):
        codes = base_v[pl.ds(start, rows), :].astype(F32).astype(BF16)
        wide = jnp.dot(codes, spread, preferred_element_type=F32)
        letter = (lax.broadcasted_iota(jnp.int32, (rows, width), 1) % 4).astype(F32)
        hot[pl.ds(start, rows), :] = jnp.where(wide == letter, 1.0, 0.0).astype(BF16)
        for col in range(0, channels, 256):
            xs[pl.ds(start, rows), pl.ds(col, 256)] = jnp.dot(
                hot[pl.ds(start, rows), :],
                table_v[:, pl.ds(col, 256)],
                preferred_element_type=F32,
            )

    own.wait()
    get_table.wait()
    embed(HALO, slab)
    to_right.wait()
    to_left.wait()
    embed(0, HALO)
    embed(HALO + slab, HALO)
    get_gains.wait()
    get_taps.wait()

    first_row = me * slab - HALO
    last_row = n * slab
    reaches = [2 * s for s in DILATIONS]
    for layer, s in enumerate(DILATIONS):
        out_lo = HALO - sum(reaches[layer + 1 :])
        out_rows = full - 2 * out_lo
        in_lo = (out_lo - reaches[layer]) // CHUNK * CHUNK
        in_rows = full - 2 * in_lo

        def norm_step(i, _, in_lo=in_lo):
            r = pl.multiple_of(in_lo + i * CHUNK, CHUNK)
            rows = xs[pl.ds(r, CHUNK), :]
            mean = jnp.sum(rows * rows, axis=1, keepdims=True) * (1.0 / channels)
            place = first_row + r + lax.broadcasted_iota(jnp.int32, (CHUNK, 1), 0)
            inside = jnp.logical_and(place >= 0, place < last_row)
            scale = jnp.where(inside, lax.rsqrt(mean + 1e-6), 0.0)
            nrm[pl.ds(r, CHUNK), :] = rows * scale
            return 0

        lax.fori_loop(0, in_rows // CHUNK, norm_step, 0)

        scaled = taps_v[layer] * gains_v[pl.ds(layer, 1), :]

        def conv_step(i, _, out_lo=out_lo, s=s, scaled=scaled):
            r = i * CHUNK
            for col in range(0, channels, 128):
                total = None
                if s % 8:
                    low = (out_lo - 2 * s) // 8 * 8
                    lead = out_lo - 2 * s - low
                    span = -(-(lead + CHUNK + 4 * s) // 8) * 8
                    near = nrm[pl.ds(pl.multiple_of(r + low, 8), span), pl.ds(col, 128)]
                for t in range(KW):
                    if s % 8:
                        part = near[lead + t * s : lead + t * s + CHUNK]
                    else:
                        place = pl.multiple_of(r + (out_lo + (t - 2) * s), 8)
                        part = nrm[pl.ds(place, CHUNK), pl.ds(col, 128)]
                    term = part * scaled[t : t + 1, col : col + 128]
                    total = term if total is None else total + term
                act[pl.ds(pl.multiple_of(r, CHUNK), CHUNK), pl.ds(col, 128)] = gelu(total).astype(
                    BF16
                )
            return 0

        lax.fori_loop(0, out_rows // CHUNK, conv_step, 0)

        get_point[layer].wait()
        for col in range(0, channels, 256):
            mixed = xs[pl.ds(out_lo, out_rows), pl.ds(col, 256)] + jnp.dot(
                act[pl.ds(0, out_rows), :],
                point_v[layer, :, pl.ds(col, 256)],
                preferred_element_type=F32,
            )
            if layer < 2:
                xs[pl.ds(out_lo, out_rows), pl.ds(col, 256)] = mixed
            else:
                trunk_v[:, pl.ds(col, 256)] = mixed.astype(BF16)

    put_trunk = pltpu.make_async_copy(trunk_v, trunk_out, local_sem.at[9])
    put_trunk.start()
    group = lax.broadcasted_iota(jnp.int32, (pool_rows, slab), 1) // POOL
    pooler = jnp.where(
        group == lax.broadcasted_iota(jnp.int32, (pool_rows, slab), 0), 1.0 / POOL, 0.0
    ).astype(BF16)
    pooled = jnp.dot(pooler, trunk_v[...], preferred_element_type=F32).astype(BF16)
    get_qw.wait()
    get_kw.wait()
    mine = pl.ds(pl.multiple_of(me * pool_rows, pool_rows), pool_rows)
    kq[mine, 0:128] = jnp.dot(pooled, qw_v[...], preferred_element_type=F32).astype(BF16)
    kq[mine, 128:256] = jnp.dot(pooled, kw_v[...], preferred_element_type=F32).astype(BF16)

    copies = []
    for d in range(1, n):
        copies.append(
            pltpu.make_async_remote_copy(
                src_ref=kq.at[mine],
                dst_ref=kq.at[mine],
                send_sem=send_sem.at[d - 1],
                recv_sem=recv_sem.at[d - 1],
                device_id={"seq": lax.rem(me + d, n)},
                device_id_type=MESH,
            )
        )
        copies[-1].start()
    for copy in copies:
        copy.wait()
    put_trunk.wait()


def pair_kernel_body(n, block, kq, weight, trunk_in, pair_out, trunk_out, w32, keys3, keysf, qrows, qcols, sem):
    step = pl.program_id(0)
    steps = pl.num_programs(0)
    width = kq.shape[0]
    pool_rows = width // n
    me = lax.axis_index("seq")

    @pl.when(step == 0)
    def _():
        pltpu.make_async_copy(trunk_in, trunk_out, sem).start()
        w32[...] = weight[...].astype(F32)
        keys = kq[:, 128:256].astype(F32)
        keysf[...] = keys
        zero = jnp.zeros((1, 128), F32)
        keys3[:, 0:128] = jnp.concatenate([zero, keys[:-1]], axis=0).astype(BF16)
        keys3[:, 128:256] = keys.astype(BF16)
        keys3[:, 256:384] = jnp.concatenate([keys[1:], zero], axis=0).astype(BF16)
        start = me * pool_rows
        before = pl.multiple_of(jnp.maximum(start - 16, 0), 16)
        after = pl.multiple_of(jnp.minimum(start + pool_rows, width - 16), 16)
        start = pl.multiple_of(start, 16)
        above = jnp.where(me > 0, kq[pl.ds(before, 16), 0:128].astype(F32), 0.0)
        below = jnp.where(me < n - 1, kq[pl.ds(after, 16), 0:128].astype(F32), 0.0)
        middle = kq[pl.ds(start, pool_rows), 0:128].astype(F32)
        rows = jnp.concatenate(
            [above[15:16], middle, below[0:1], jnp.zeros((126 - pool_rows, 128), F32)], axis=0
        )
        qrows[...] = rows[0 : qrows.shape[0]]
        cols = rows.T
        for i in range(pool_rows + 2):
            qcols[i] = jnp.broadcast_to(cols[:, i : i + 1], (128, 128))

    for half in range(block // 2):
        base = step * block + half * 2
        kernels = []
        for k in range(2):
            parts = []
            for b in range(3):
                parts.append(
                    (
                        qcols[base + k] * w32[0, b]
                        + qcols[base + k + 1] * w32[1, b]
                        + qcols[base + k + 2] * w32[2, b]
                    ).astype(BF16)
                )
            kernels.append(jnp.concatenate(parts, axis=0))
        conv = jnp.dot(
            keys3[...], jnp.concatenate(kernels, axis=1), preferred_element_type=F32
        )
        for k in range(2):
            pair = (keysf[...] * qrows[pl.ds(base + k + 1, 1), :]).astype(BF16).astype(F32)
            pair_out[half * 2 + k] = (pair + gelu(conv[:, k * 128 : k * 128 + 128])).astype(BF16)

    @pl.when(step == steps - 1)
    def _():
        pltpu.make_async_copy(trunk_in, trunk_out, sem).wait()


def on_device(
    n, bases, embed_table, norm_gains, depth_taps, point_weight, query_weight, key_weight, pair_kernel
):
    slab = bases.shape[0]
    channels = embed_table.shape[1]
    full = slab + 2 * HALO
    pool_rows = slab // POOL
    width = pool_rows * n
    any_spec = pl.BlockSpec(memory_space=pl.ANY)
    vmem_spec = pl.BlockSpec(memory_space=pltpu.VMEM)
    trunk, kq = pl.pallas_call(
        functools.partial(trunk_kernel, n),
        out_shape=(
            jax.ShapeDtypeStruct((slab, channels), BF16),
            jax.ShapeDtypeStruct((width, 256), BF16),
        ),
        in_specs=[any_spec] * 7,
        out_specs=(any_spec, vmem_spec),
        scratch_shapes=[
            pltpu.VMEM((full, bases.shape[1]), jnp.int32),
            pltpu.VMEM(embed_table.shape, BF16),
            pltpu.VMEM(norm_gains.shape, F32),
            pltpu.VMEM(depth_taps.shape, F32),
            pltpu.VMEM(point_weight.shape, BF16),
            pltpu.VMEM(query_weight.shape, BF16),
            pltpu.VMEM(key_weight.shape, BF16),
            pltpu.VMEM((full, embed_table.shape[0]), BF16),
            pltpu.VMEM((full, channels), F32),
            pltpu.VMEM((full, channels), F32),
            pltpu.VMEM((full, channels), BF16),
            pltpu.VMEM((slab, channels), BF16),
            pltpu.SemaphoreType.DMA((10,)),
            pltpu.SemaphoreType.DMA((2,)),
            pltpu.SemaphoreType.DMA((2,)),
            pltpu.SemaphoreType.DMA((n - 1,)),
            pltpu.SemaphoreType.DMA((n - 1,)),
        ],
        compiler_params=pltpu.CompilerParams(
            collective_id=0, has_side_effects=True, vmem_limit_bytes=40 * 1024 * 1024
        ),
        name="trunk_and_gather",
    )(bases, embed_table, norm_gains, depth_taps, point_weight, query_weight, key_weight)

    block = 4
    pair_map, trunk = pl.pallas_call(
        functools.partial(pair_kernel_body, n, block),
        grid=(pool_rows // block,),
        out_shape=(
            jax.ShapeDtypeStruct((pool_rows, width, 128), BF16),
            jax.ShapeDtypeStruct((slab, channels), BF16),
        ),
        in_specs=[
            pl.BlockSpec((width, 256), lambda i: (0, 0)),
            pl.BlockSpec((3, 3, 128, 128), lambda i: (0, 0, 0, 0)),
            any_spec,
        ],
        out_specs=(pl.BlockSpec((block, width, 128), lambda i: (i, 0, 0)), any_spec),
        scratch_shapes=[
            pltpu.VMEM((3, 3, 128, 128), F32),
            pltpu.VMEM((width, 384), BF16),
            pltpu.VMEM((width, 128), F32),
            pltpu.VMEM((pool_rows + 8, 128), F32),
            pltpu.VMEM((pool_rows + 2, 128, 128), F32),
            pltpu.SemaphoreType.DMA,
        ],
        compiler_params=pltpu.CompilerParams(vmem_limit_bytes=40 * 1024 * 1024),
        name="pair_map",
    )(kq, pair_kernel, trunk)
    return (trunk, pair_map)


def solution(mesh):
    return jax.shard_map(
        functools.partial(on_device, mesh.shape["seq"]),
        mesh=mesh,
        in_specs=(P(("batch", "seq"), None), P(), P(), P(), P(), P(), P(), P()),
        out_specs=(P(("batch", "seq"), None), P(("batch", "seq"), None, None)),
        check_vma=False,
    )
```

time: 122 us -> 47.3 us (0.39)
  the two profiles are of different devices: /device:TPU:1 before, /device:TPU:0 now
where the time goes in v1:
time: 47.3 us; the launch traced here: 46.9 us
  Pallas kernels  38.7 us (82%)
  local copies, waits for them, and re-layouts  7.49 us (16%)
  between operations  0.66 us (1%)
    pallas_call x1, Pallas kernels, on_device(): pl.pallas_call(functools.partial(trunk_kernel, n), out_shape=(jax.ShapeDt...  30.7 us
    pallas_call x1, Pallas kernels, on_device(): pl.pallas_call(functools.partial(pair_kernel_body, n, block), grid=(pool_...  8.01 us
    unnamed x15, local copies, waits for them, and re-layouts  7.49 us

profile of v1, /device:TPU:0, one launch (start us, length us, event | category | flops | bytes accessed | tf_op | source)
XLA Modules:
  0.0 46.9 jit_solution(1423010291450275930)
XLA Ops:
  0.6 0.8 %copy.10.taps = f32[3,5,768]{2,1,0:T(8,128)S(1)} copy(f32[3,5,768]{2,0,1:T(4,128)} %param.11) | data formatting | bytes 92160 | tf_op args[3]
  1.5 0.0 copy-start
  1.5 2.0 %copy-done = bf16[3,768,768]{2,1,0:T(8,128)(2,1)S(1)} copy-done((bf16[3,768,768]{2,1,0:T(8,128)(2,1)S(1)}, bf16[3,768,768]{2,1,0:T(8,128)(2,1)}, u32[]{:S(2)}) %copy-start) | copy-done | bytes 3538968
  3.5 0.0 copy-start.1
  3.5 1.1 %copy-done.1 = bf16[512,768]{1,0:T(8,128)(2,1)S(1)} copy-done((bf16[512,768]{1,0:T(8,128)(2,1)S(1)}, bf16[512,768]{1,0:T(8,128)(2,1)}, u32[]{:S(2)}) %copy-start.1) | copy-done | bytes 786456
  4.6 0.0 copy-start.3
  4.6 0.9 %copy-done.3 = s32[512,128]{1,0:T(8,128)S(1)} copy-done((s32[512,128]{1,0:T(8,128)S(1)}, s32[512,128]{1,0:T(8,128)}, u32[]{:S(2)}) %copy-start.3) | copy-done | bytes 262168
  5.6 0.0 copy-start.4
  5.6 0.9 %copy-done.4 = bf16[768,128]{1,0:T(8,128)(2,1)S(1)} copy-done((bf16[768,128]{1,0:T(8,128)(2,1)S(1)}, bf16[768,128]{1,0:T(8,128)(2,1)}, u32[]{:S(2)}) %copy-start.4) | copy-done | bytes 196632
  6.5 0.0 copy-start.5
  6.5 0.9 %copy-done.5 = bf16[768,128]{1,0:T(8,128)(2,1)S(1)} copy-done((bf16[768,128]{1,0:T(8,128)(2,1)S(1)}, bf16[768,128]{1,0:T(8,128)(2,1)}, u32[]{:S(2)}) %copy-start.5) | copy-done | bytes 196632
  7.4 0.0 copy-start.6
  7.4 0.7 %copy-done.6 = f32[3,768]{1,0:T(4,128)S(1)} copy-done((f32[3,768]{1,0:T(4,128)S(1)}, f32[3,768]{1,0:T(4,128)}, u32[]{:S(2)}) %copy-start.6) | copy-done | bytes 9240
  8.1 0.0 copy-start.2
  8.1 30.7 %trunk_and_gather.1 = (bf16[512,768]{1,0:T(8,128)(2,1)S(1)}, bf16[512,256]{1,0:T(8,128)(2,1)S(1)}) custom-call(s32[512,128]{1,0:T(8,128)S(1)} %copy-done.3, bf16[512,768]{1,0:T(8,128)(2,1)S(1)} %copy-done.1, f32[3,768]{1,0:T(4,128)S(1)} %copy-done.6, f32[3,5,768]{2,1,0:T(8,128)S(1)} %copy.10.taps, bf16[3,768,768]{2,1,0:T(8,128)(2,1)S(1)} %copy-done, ...), custom_call_target="tpu_custom_call" | custom-call | tf_op jit(solution)/shard_map/trunk_and_gather/pallas_call | solution.py:296
  38.9 0.0 copy-done.2
  38.9 8.0 %pair_map.1 = (bf16[32,512,128]{2,1,0:T(8,128)(2,1)}, bf16[512,768]{1,0:T(8,128)(2,1)}) custom-call(bf16[512,256]{1,0:T(8,128)(2,1)S(1)} %get-tuple-element.6.kq, bf16[3,3,128,128]{3,2,1,0:T(8,128)(2,1)S(1)} %copy-done.2, bf16[512,768]{1,0:T(8,128)(2,1)S(1)} %get-tuple-element.7.trunk_in), custom_call_target="tpu_custom_call" | custom-call | tf_op jit(solution)/shard_map/pair_map/pallas_call | solution.py:330
Async XLA Ops:
  1.5 2.0 %copy-start = (bf16[3,768,768]{2,1,0:T(8,128)(2,1)S(1)}, bf16[3,768,768]{2,1,0:T(8,128)(2,1)}, u32[]{:S(2)}) copy-start(bf16[3,768,768]{2,1,0:T(8,128)(2,1)} %point.1) | copy-start | bytes 10616836
  3.5 1.1 %copy-start.1 = (bf16[512,768]{1,0:T(8,128)(2,1)S(1)}, bf16[512,768]{1,0:T(8,128)(2,1)}, u32[]{:S(2)}) copy-start(bf16[512,768]{1,0:T(8,128)(2,1)} %table.1) | copy-start | bytes 2359300
  4.6 0.9 %copy-start.3 = (s32[512,128]{1,0:T(8,128)S(1)}, s32[512,128]{1,0:T(8,128)}, u32[]{:S(2)}) copy-start(s32[512,128]{1,0:T(8,128)} %bases.1) | copy-start | bytes 786436
  5.6 0.9 %copy-start.4 = (bf16[768,128]{1,0:T(8,128)(2,1)S(1)}, bf16[768,128]{1,0:T(8,128)(2,1)}, u32[]{:S(2)}) copy-start(bf16[768,128]{1,0:T(8,128)(2,1)} %query_w.1) | copy-start | bytes 589828
  6.5 0.9 %copy-start.5 = (bf16[768,128]{1,0:T(8,128)(2,1)S(1)}, bf16[768,128]{1,0:T(8,128)(2,1)}, u32[]{:S(2)}) copy-start(bf16[768,128]{1,0:T(8,128)(2,1)} %key_w.1) | copy-start | bytes 589828
  7.4 0.7 %copy-start.6 = (f32[3,768]{1,0:T(4,128)S(1)}, f32[3,768]{1,0:T(4,128)}, u32[]{:S(2)}) copy-start(f32[3,768]{1,0:T(4,128)} %gains.1) | copy-start | bytes 27652
  8.1 30.7 %copy-start.2 = (bf16[3,3,128,128]{3,2,1,0:T(8,128)(2,1)S(1)}, bf16[3,3,128,128]{3,2,1,0:T(8,128)(2,1)}, u32[]{:S(2)}) copy-start(bf16[3,3,128,128]{3,2,1,0:T(8,128)(2,1)} %weight.1) | copy-start | bytes 884740

commit v2 on v1

v2 whole, which is shorter than its diff:
```python
import functools

import jax
import jax.numpy as jnp
from jax import lax
from jax.experimental import pallas as pl
from jax.experimental.pallas import tpu as pltpu
from jax.sharding import PartitionSpec as P

KW = 5
DILATIONS = (2, 8, 32)
POOL = 16
HALO = 96
CHUNK = 32
GELU_A = 0.7978845608028654
GELU_B = 0.7978845608028654 * 0.044715
MESH = pl.DeviceIdType.MESH
F32 = jnp.float32
BF16 = jnp.bfloat16


def gelu(v):
    half = 0.5 * v
    return half + half * jnp.tanh(v * (GELU_A + GELU_B * (v * v)))


def blocks_of(rows):
    units = rows // 16
    sizes = [(units + 2 - k) // 3 * 16 for k in range(3)]
    return [(sum(sizes[:k]), sizes[k]) for k in range(3)]


def pieces_of(low, rows, most):
    return [(low + at, min(most, rows - at)) for at in range(0, rows, most)]


def interleave(first, second):
    count = max(len(first), len(second), 1)
    done = [0, 0]
    for k in range(count):
        for which, tasks in enumerate((first, second)):
            target = len(tasks) * (k + 1) // count
            while done[which] < target:
                tasks[done[which]]()
                done[which] += 1


def trunk_kernel(
    n,
    bases,
    table,
    gains,
    taps,
    point,
    query_w,
    key_w,
    trunk_out,
    keys,
    queries,
    base_v,
    table_v,
    gains_v,
    taps_v,
    point_v,
    qw_v,
    kw_v,
    hot,
    xs,
    nrm,
    act,
    trunk_v,
    local_sem,
    halo_send,
    halo_recv,
    query_send,
    query_recv,
    send_sem,
    recv_sem,
):
    slab = bases.shape[0]
    channels = table.shape[1]
    full = slab + 2 * HALO
    pool_rows = slab // POOL
    me = lax.axis_index("seq")
    right = lax.rem(me + 1, n)
    left = lax.rem(me + n - 1, n)

    barrier = pltpu.get_barrier_semaphore()
    for d in range(1, n):
        pl.semaphore_signal(
            barrier, inc=1, device_id={"seq": lax.rem(me + d, n)}, device_id_type=MESH
        )

    def fetch(source, target, k):
        copy = pltpu.make_async_copy(source, target, local_sem.at[k])
        copy.start()
        return copy

    own = fetch(bases, base_v.at[pl.ds(HALO, slab)], 0)
    get_table = fetch(table, table_v, 1)
    weights = [fetch(gains, gains_v, 2), fetch(taps, taps_v, 3)]
    for layer in range(3):
        weights.append(fetch(point.at[layer], point_v.at[layer], 4 + layer))
    weights.append(fetch(query_w, qw_v, 7))
    weights.append(fetch(key_w, kw_v, 8))

    width = table.shape[0]
    places = width // 4
    spread = (
        lax.broadcasted_iota(jnp.int32, (places, width), 1) // 4
        == lax.broadcasted_iota(jnp.int32, (places, width), 0)
    ).astype(BF16)
    letter = (lax.broadcasted_iota(jnp.int32, (1, width), 1) % 4).astype(F32)

    def one_hot(start, rows):
        codes = base_v[pl.ds(start, rows), :].astype(F32).astype(BF16)
        wide = jnp.dot(codes, spread, preferred_element_type=F32)
        hot[pl.ds(start, rows), :] = jnp.where(wide == letter, 1.0, 0.0).astype(BF16)

    def embed(start, rows):
        for col in range(0, channels, 256):
            xs[pl.ds(start, rows), pl.ds(col, 256)] = jnp.dot(
                hot[pl.ds(start, rows), :],
                table_v[:, pl.ds(col, 256)],
                preferred_element_type=F32,
            )

    own.wait()
    one_hot(HALO, slab)
    pl.semaphore_wait(barrier, n - 1)
    to_right = pltpu.make_async_remote_copy(
        src_ref=bases.at[pl.ds(slab - HALO, HALO)],
        dst_ref=base_v.at[pl.ds(0, HALO)],
        send_sem=halo_send.at[0],
        recv_sem=halo_recv.at[0],
        device_id={"seq": right},
        device_id_type=MESH,
    )
    to_right.start()
    to_left = pltpu.make_async_remote_copy(
        src_ref=bases.at[pl.ds(0, HALO)],
        dst_ref=base_v.at[pl.ds(HALO + slab, HALO)],
        send_sem=halo_send.at[1],
        recv_sem=halo_recv.at[1],
        device_id={"seq": left},
        device_id_type=MESH,
    )
    to_left.start()

    first_row = me * slab - HALO
    last_row = n * slab
    reaches = [2 * s for s in DILATIONS]
    lows = [HALO - sum(reaches[layer + 1 :]) for layer in range(3)]
    scaled = []

    def norm_piece(layer, r, rows):
        floats = xs[pl.ds(r, rows), :]
        mean = jnp.sum(floats * floats, axis=1, keepdims=True) * (1.0 / channels)
        scale = lax.rsqrt(mean + 1e-6)
        if r < HALO or r + rows > HALO + slab:
            place = first_row + r + lax.broadcasted_iota(jnp.int32, (rows, 1), 0)
            inside = jnp.logical_and(place >= 0, place < last_row)
            scale = jnp.where(inside, scale, 0.0)
        nrm[layer % 2, pl.ds(r, rows), :] = (floats * scale).astype(BF16)

    def norms(layer, low, rows):
        return [
            functools.partial(norm_piece, layer, r, size) for r, size in pieces_of(low, rows, 32)
        ]

    def conv_piece(layer, r, rows, col):
        s = DILATIONS[layer]
        total = None
        low = (r - 2 * s) // 16 * 16
        span = -(-(r + rows + 2 * s - low) // 16) * 16
        if s % 16:
            near = nrm[layer % 2, pl.ds(low, span), pl.ds(col, 128)]
        for t in range(KW):
            at = r + (t - 2) * s
            if s % 16:
                part = near[at - low : at - low + rows]
            else:
                part = nrm[layer % 2, pl.ds(at, rows), pl.ds(col, 128)]
            term = part * scaled[layer][t : t + 1, col : col + 128]
            total = term if total is None else total + term
        act[layer % 2, pl.ds(r, rows), pl.ds(col, 128)] = gelu(total)

    def convs(layer, k):
        at, size = blocks_of(full - 2 * lows[layer])[k]
        return [
            functools.partial(conv_piece, layer, r, rows, col)
            for r, rows in pieces_of(lows[layer] + at, size, 32)
            for col in range(0, channels, 128)
        ]

    def mix_piece(layer, r, rows, col):
        mixed = xs[pl.ds(r, rows), pl.ds(col, 256)] + jnp.dot(
            act[layer % 2, pl.ds(r, rows), :],
            point_v[layer, :, pl.ds(col, 256)],
            preferred_element_type=F32,
        )
        if layer < 2:
            xs[pl.ds(r, rows), pl.ds(col, 256)] = mixed
        else:
            trunk_v[pl.ds(r - HALO, rows), pl.ds(col, 256)] = mixed.astype(BF16)

    def mixes(layer, k):
        at, size = blocks_of(full - 2 * lows[layer])[k]
        return [
            functools.partial(mix_piece, layer, lows[layer] + at, size, col)
            for col in range(0, channels, 256)
        ]

    def next_norms(layer, k):
        if layer == 2:
            return []
        at, size = blocks_of(full - 2 * lows[layer])[k]
        return norms(layer + 1, lows[layer] + at, size)

    get_table.wait()
    for at in range(0, slab, slab // 2):
        embed(HALO + at, slab // 2)
    for task in norms(0, HALO, slab):
        task()
    to_right.wait()
    to_left.wait()
    for start in (0, HALO + slab):
        one_hot(start, HALO)
        embed(start, HALO)
    for weight in weights:
        weight.wait()
    for layer in range(3):
        scaled.append((taps_v[:, layer] * gains_v[pl.ds(layer, 1), :]).astype(BF16))
    for task in norms(0, 0, HALO) + norms(0, HALO + slab, HALO):
        task()

    interleave(convs(0, 0), [])
    for layer in range(3):
        interleave(mixes(layer, 0), convs(layer, 1))
        interleave(mixes(layer, 1), next_norms(layer, 0) + convs(layer, 2))
        following = convs(layer + 1, 0) if layer < 2 else []
        interleave(mixes(layer, 2), next_norms(layer, 1) + following)
        interleave([], next_norms(layer, 2))

    put_trunk = pltpu.make_async_copy(trunk_v, trunk_out, local_sem.at[9])
    put_trunk.start()
    group = lax.broadcasted_iota(jnp.int32, (pool_rows, slab), 1) // POOL
    pooler = jnp.where(
        group == lax.broadcasted_iota(jnp.int32, (pool_rows, slab), 0), 1.0 / POOL, 0.0
    ).astype(BF16)
    pooled = jnp.dot(pooler, trunk_v[...], preferred_element_type=F32).astype(BF16)
    mine = pl.ds(pl.multiple_of(me * pool_rows, pool_rows), pool_rows)
    keys[mine, :] = jnp.dot(pooled, kw_v[...], preferred_element_type=F32).astype(BF16)

    copies = []
    for d in sorted(range(1, n), key=lambda d: -min(d, n - d)):
        copies.append(
            pltpu.make_async_remote_copy(
                src_ref=keys.at[mine],
                dst_ref=keys.at[mine],
                send_sem=send_sem.at[d - 1],
                recv_sem=recv_sem.at[d - 1],
                device_id={"seq": lax.rem(me + d, n)},
                device_id_type=MESH,
            )
        )
        copies[-1].start()
    queries[pl.ds(16, pool_rows), :] = jnp.dot(
        pooled, qw_v[...], preferred_element_type=F32
    ).astype(BF16)
    for k, (source, target, peer) in enumerate(
        ((pool_rows, 0, right), (16, 16 + pool_rows, left))
    ):
        copies.append(
            pltpu.make_async_remote_copy(
                src_ref=queries.at[pl.ds(source, 16)],
                dst_ref=queries.at[pl.ds(target, 16)],
                send_sem=query_send.at[k],
                recv_sem=query_recv.at[k],
                device_id={"seq": peer},
                device_id_type=MESH,
            )
        )
        copies[-1].start()
    for copy in copies:
        copy.wait()
    put_trunk.wait()


def pair_kernel_body(
    n, block, keys, queries, weight, trunk_in, pair_out, trunk_out, keys3, qrows, qcols, sem
):
    step = pl.program_id(0)
    steps = pl.num_programs(0)
    width = keys.shape[0]
    pool_rows = width // n
    me = lax.axis_index("seq")

    @pl.when(step == 0)
    def _():
        pltpu.make_async_copy(trunk_in, trunk_out, sem).start()
        floats = keys[...].astype(F32)
        zero = jnp.zeros((1, 128), F32)
        keys3[:, 0:128] = jnp.concatenate([zero, floats[:-1]], axis=0).astype(BF16)
        keys3[:, 128:256] = keys[...]
        keys3[:, 256:384] = jnp.concatenate([floats[1:], zero], axis=0).astype(BF16)
        rows = queries[...].astype(F32)
        above = jnp.where(me > 0, rows[15:16], 0.0)
        below = jnp.where(me < n - 1, rows[16 + pool_rows : 17 + pool_rows], 0.0)
        rows = jnp.concatenate(
            [above, rows[16 : 16 + pool_rows], below, jnp.zeros((126 - pool_rows, 128), F32)],
            axis=0,
        )
        qrows[...] = rows[0 : qrows.shape[0]]
        cols = rows.T
        for i in range(pool_rows + 2):
            qcols[i] = jnp.broadcast_to(cols[:, i : i + 1], (128, 128)).astype(BF16)

    for half in range(block // 2):
        base = step * block + half * 2
        kernels = []
        for k in range(2):
            parts = []
            for b in range(3):
                parts.append(
                    qcols[base + k] * weight[0, b]
                    + qcols[base + k + 1] * weight[1, b]
                    + qcols[base + k + 2] * weight[2, b]
                )
            kernels.append(jnp.concatenate(parts, axis=0))
        conv = jnp.dot(
            keys3[...], jnp.concatenate(kernels, axis=1), preferred_element_type=F32
        ).astype(BF16)
        for k in range(2):
            row = jnp.broadcast_to(qrows[pl.ds(base + k + 1, 1), :], (16, 128)).astype(BF16)
            pair = (keys[...].reshape(width // 16, 16, 128) * row[None]).reshape(width, 128)
            pair_out[half * 2 + k] = pair + gelu(conv[:, k * 128 : k * 128 + 128])

    @pl.when(step == steps - 1)
    def _():
        pltpu.make_async_copy(trunk_in, trunk_out, sem).wait()


def on_device(
    n, bases, embed_table, norm_gains, depth_taps, point_weight, query_weight, key_weight, pair_kernel
):
    slab = bases.shape[0]
    channels = embed_table.shape[1]
    full = slab + 2 * HALO
    pool_rows = slab // POOL
    width = pool_rows * n
    hbm_spec = pl.BlockSpec(memory_space=pltpu.HBM)
    vmem_spec = pl.BlockSpec(memory_space=pltpu.VMEM)
    trunk, keys, queries = pl.pallas_call(
        functools.partial(trunk_kernel, n),
        out_shape=(
            jax.ShapeDtypeStruct((slab, channels), BF16),
            jax.ShapeDtypeStruct((width, 128), BF16),
            jax.ShapeDtypeStruct((pool_rows + 32, 128), BF16),
        ),
        in_specs=[hbm_spec] * 7,
        out_specs=(hbm_spec, vmem_spec, vmem_spec),
        scratch_shapes=[
            pltpu.VMEM((full, bases.shape[1]), jnp.int32),
            pltpu.VMEM(embed_table.shape, BF16),
            pltpu.VMEM(norm_gains.shape, F32),
            pltpu.VMEM((KW, 3, channels), F32),
            pltpu.VMEM(point_weight.shape, BF16),
            pltpu.VMEM(query_weight.shape, BF16),
            pltpu.VMEM(key_weight.shape, BF16),
            pltpu.VMEM((full, embed_table.shape[0]), BF16),
            pltpu.VMEM((full, channels), F32),
            pltpu.VMEM((2, full, channels), BF16),
            pltpu.VMEM((2, full, channels), BF16),
            pltpu.VMEM((slab, channels), BF16),
            pltpu.SemaphoreType.DMA((10,)),
            pltpu.SemaphoreType.DMA((2,)),
            pltpu.SemaphoreType.DMA((2,)),
            pltpu.SemaphoreType.DMA((2,)),
            pltpu.SemaphoreType.DMA((2,)),
            pltpu.SemaphoreType.DMA((n - 1,)),
            pltpu.SemaphoreType.DMA((n - 1,)),
        ],
        compiler_params=pltpu.CompilerParams(
            collective_id=0, has_side_effects=True, vmem_limit_bytes=63 * 1024 * 1024
        ),
        name="trunk_and_gather",
    )(bases, embed_table, norm_gains, depth_taps.swapaxes(0, 1), point_weight, query_weight, key_weight)

    block = 4
    pair_map, trunk = pl.pallas_call(
        functools.partial(pair_kernel_body, n, block),
        grid=(pool_rows // block,),
        out_shape=(
            jax.ShapeDtypeStruct((pool_rows, width, 128), BF16),
            jax.ShapeDtypeStruct((slab, channels), BF16),
        ),
        in_specs=[
            pl.BlockSpec((width, 128), lambda i: (0, 0)),
            pl.BlockSpec((pool_rows + 32, 128), lambda i: (0, 0)),
            pl.BlockSpec((3, 3, 128, 128), lambda i: (0, 0, 0, 0)),
            hbm_spec,
        ],
        out_specs=(pl.BlockSpec((block, width, 128), lambda i: (i, 0, 0)), hbm_spec),
        scratch_shapes=[
            pltpu.VMEM((width, 384), BF16),
            pltpu.VMEM((pool_rows + 8, 128), F32),
            pltpu.VMEM((pool_rows + 2, 128, 128), BF16),
            pltpu.SemaphoreType.DMA,
        ],
        compiler_params=pltpu.CompilerParams(vmem_limit_bytes=63 * 1024 * 1024),
        name="pair_map",
    )(keys, queries, pair_kernel, trunk)
    return (trunk, pair_map)


def solution(mesh):
    return jax.shard_map(
        functools.partial(on_device, mesh.shape["seq"]),
        mesh=mesh,
        in_specs=(P(("batch", "seq"), None), P(), P(), P(), P(), P(), P(), P()),
        out_specs=(P(("batch", "seq"), None), P(("batch", "seq"), None, None)),
        check_vma=False,
    )
```

time: 47.3 us -> 51 us (1.078)
  Pallas kernels: 38.7 us -> 50.2 us
  local copies, waits for them, and re-layouts: 7.49 us -> 0 us
    pallas_call x1, Pallas kernels: 8.01 us -> 26.8 us  [on_device(): pl.pallas_call(functools.partial(pair_kernel_body, n, block), grid=(pool_...]
    unnamed x15 -> x0, local copies, waits for them, and re-layouts: 7.49 us -> none
    pallas_call x1, Pallas kernels: 30.7 us -> 23.4 us  [on_device(): pl.pallas_call(functools.partial(trunk_kernel, n), out_shape=(jax.ShapeDt...]
where the time goes in v2:
time: 51 us; the launch traced here: 50.9 us
  Pallas kernels  50.2 us (98%)
  between operations  0.64 us (1%)
    pallas_call x1, Pallas kernels, on_device(): pl.pallas_call(functools.partial(pair_kernel_body, n, block), grid=(pool_...  26.8 us
    pallas_call x1, Pallas kernels, on_device(): pl.pallas_call(functools.partial(trunk_kernel, n), out_shape=(jax.ShapeDt...  23.4 us

profile of v2, /device:TPU:0, one launch (start us, length us, event | category | flops | bytes accessed | tf_op | source)
XLA Modules:
  0.0 50.9 jit_solution(15531013580792498792)
XLA Ops:
  0.6 23.4 %trunk_and_gather.1 = (bf16[512,768]{1,0:T(8,128)(2,1)}, bf16[512,128]{1,0:T(8,128)(2,1)}, bf16[64,128]{1,0:T(8,128)(2,1)}) custom-call(s32[512,128]{1,0:T(8,128)} %bases.1, bf16[512,768]{1,0:T(8,128)(2,1)} %table.1, f32[3,768]{1,0:T(4,128)} %gains.1, f32[5,3,768]{2,1,0:T(4,128)} %bitcast.1, bf16[3,768,768]{2,1,0:T(8,128)(2,1)} %point.1, ...), custom_call_target="tpu_custom_call" | custom-call | tf_op jit(solution)/shard_map/trunk_and_gather/pallas_call | solution.py:354
  24.1 26.8 %pair_map.1 = (bf16[32,512,128]{2,1,0:T(8,128)(2,1)}, bf16[512,768]{1,0:T(8,128)(2,1)}) custom-call(bf16[512,128]{1,0:T(8,128)(2,1)} %get-tuple-element.7.keys, bf16[64,128]{1,0:T(8,128)(2,1)} %get-tuple-element.8.queries, bf16[3,3,128,128]{3,2,1,0:T(8,128)(2,1)} %weight.1, bf16[512,768]{1,0:T(8,128)(2,1)} %get-tuple-element.9.trunk_in), custom_call_target="tpu_custom_call" | custom-call | tf_op jit(solution)/shard_map/pair_map/pallas_call | solution.py:391

commit v3 on v2

--- a/solution.py
+++ b/solution.py
@@ -288,7 +288,7 @@
 
 
 def pair_kernel_body(
-    n, block, keys, queries, weight, trunk_in, pair_out, trunk_out, keys3, qrows, qcols, sem
+    n, block, keys, queries, weight, trunk_in, pair_out, trunk_out, keys3, qrows, qcols, trunk_v, sem
 ):
     step = pl.program_id(0)
     steps = pl.num_programs(0)
@@ -298,7 +298,7 @@
 
     @pl.when(step == 0)
     def _():
-        pltpu.make_async_copy(trunk_in, trunk_out, sem).start()
+        pltpu.make_async_copy(trunk_in, trunk_v, sem.at[0]).start()
         floats = keys[...].astype(F32)
         zero = jnp.zeros((1, 128), F32)
         keys3[:, 0:128] = jnp.concatenate([zero, floats[:-1]], axis=0).astype(BF16)
@@ -336,9 +336,14 @@
             pair = (keys[...].reshape(width // 16, 16, 128) * row[None]).reshape(width, 128)
             pair_out[half * 2 + k] = pair + gelu(conv[:, k * 128 : k * 128 + 128])
 
+    @pl.when(step == 0)
+    def _():
+        pltpu.make_async_copy(trunk_in, trunk_v, sem.at[0]).wait()
+        pltpu.make_async_copy(trunk_v, trunk_out, sem.at[1]).start()
+
     @pl.when(step == steps - 1)
     def _():
-        pltpu.make_async_copy(trunk_in, trunk_out, sem).wait()
+        pltpu.make_async_copy(trunk_v, trunk_out, sem.at[1]).wait()
 
 
 def on_device(
@@ -406,7 +411,8 @@
             pltpu.VMEM((width, 384), BF16),
             pltpu.VMEM((pool_rows + 8, 128), F32),
             pltpu.VMEM((pool_rows + 2, 128, 128), BF16),
-            pltpu.SemaphoreType.DMA,
+            pltpu.VMEM((slab, channels), BF16),
+            pltpu.SemaphoreType.DMA((2,)),
         ],
         compiler_params=pltpu.CompilerParams(vmem_limit_bytes=63 * 1024 * 1024),
         name="pair_map",

time: 51 us -> 32.7 us (0.64)
  Pallas kernels: 50.2 us -> 31.9 us
    pallas_call x1, Pallas kernels: 26.8 us -> 8.48 us  [on_device(): pl.pallas_call(functools.partial(pair_kernel_body, n, block), grid=(pool_...]
where the time goes in v3:
time: 32.7 us; the launch traced here: 32.5 us
  Pallas kernels  31.9 us (98%)
  between operations  0.64 us (2%)
    pallas_call x1, Pallas kernels, on_device(): pl.pallas_call(functools.partial(trunk_kernel, n), out_shape=(jax.ShapeDt...  23.4 us
    pallas_call x1, Pallas kernels, on_device(): pl.pallas_call(functools.partial(pair_kernel_body, n, block), grid=(pool_...  8.48 us

profile of v3, /device:TPU:0, one launch (start us, length us, event | category | flops | bytes accessed | tf_op | source)
XLA Modules:
  0.0 32.5 jit_solution(1409041825080865697)
XLA Ops:
  0.6 23.4 %trunk_and_gather.1 = (bf16[512,768]{1,0:T(8,128)(2,1)}, bf16[512,128]{1,0:T(8,128)(2,1)}, bf16[64,128]{1,0:T(8,128)(2,1)}) custom-call(s32[512,128]{1,0:T(8,128)} %bases.1, bf16[512,768]{1,0:T(8,128)(2,1)} %table.1, f32[3,768]{1,0:T(4,128)} %gains.1, f32[5,3,768]{2,1,0:T(4,128)} %bitcast.1, bf16[3,768,768]{2,1,0:T(8,128)(2,1)} %point.1, ...), custom_call_target="tpu_custom_call" | custom-call | tf_op jit(solution)/shard_map/trunk_and_gather/pallas_call | solution.py:359
  24.1 8.5 %pair_map.1 = (bf16[32,512,128]{2,1,0:T(8,128)(2,1)}, bf16[512,768]{1,0:T(8,128)(2,1)}) custom-call(bf16[512,128]{1,0:T(8,128)(2,1)} %get-tuple-element.7.keys, bf16[64,128]{1,0:T(8,128)(2,1)} %get-tuple-element.8.queries, bf16[3,3,128,128]{3,2,1,0:T(8,128)(2,1)} %weight.1, bf16[512,768]{1,0:T(8,128)(2,1)} %get-tuple-element.9.trunk_in), custom_call_target="tpu_custom_call" | custom-call | tf_op jit(solution)/shard_map/pair_map/pallas_call | solution.py:396

commit v4 on v3

--- a/solution.py
+++ b/solution.py
@@ -54,9 +54,11 @@
     point,
     query_w,
     key_w,
+    weight,
     trunk_out,
     keys,
     queries,
+    weff,
     base_v,
     table_v,
     gains_v,
@@ -64,6 +66,8 @@
     point_v,
     qw_v,
     kw_v,
+    weight_v,
+    qcols,
     hot,
     xs,
     nrm,
@@ -103,6 +107,7 @@
         weights.append(fetch(point.at[layer], point_v.at[layer], 4 + layer))
     weights.append(fetch(query_w, qw_v, 7))
     weights.append(fetch(key_w, kw_v, 8))
+    weights.append(fetch(weight, weight_v, 10))
 
     width = table.shape[0]
     places = width // 4
@@ -189,7 +194,7 @@
         at, size = blocks_of(full - 2 * lows[layer])[k]
         return [
             functools.partial(conv_piece, layer, r, rows, col)
-            for r, rows in pieces_of(lows[layer] + at, size, 32)
+            for r, rows in pieces_of(lows[layer] + at, size, 112)
             for col in range(0, channels, 128)
         ]
 
@@ -265,9 +270,8 @@
             )
         )
         copies[-1].start()
-    queries[pl.ds(16, pool_rows), :] = jnp.dot(
-        pooled, qw_v[...], preferred_element_type=F32
-    ).astype(BF16)
+    own_queries = jnp.dot(pooled, qw_v[...], preferred_element_type=F32).astype(BF16)
+    queries[pl.ds(16, pool_rows), :] = own_queries
     for k, (source, target, peer) in enumerate(
         ((pool_rows, 0, right), (16, 16 + pool_rows, left))
     ):
@@ -282,19 +286,43 @@
             )
         )
         copies[-1].start()
-    for copy in copies:
+
+    def spread_rows(rows, places):
+        short = 128 - rows.shape[0]
+        cols = jnp.concatenate([rows, jnp.zeros((short, 128), F32)], axis=0).T
+        for source, target in places:
+            qcols[target] = jnp.broadcast_to(cols[:, source : source + 1], (128, 128)).astype(BF16)
+
+    def combine(i):
+        for b in range(3):
+            weff[i // 2, pl.ds(b * 128, 128), pl.ds(i % 2 * 128, 128)] = (
+                qcols[i] * weight_v[0, b]
+                + qcols[i + 1] * weight_v[1, b]
+                + qcols[i + 2] * weight_v[2, b]
+            )
+
+    spread_rows(own_queries.astype(F32), [(i, i + 1) for i in range(pool_rows)])
+    for i in range(1, pool_rows - 1):
+        combine(i)
+    for copy in copies[-2:]:
+        copy.wait()
+    above = jnp.where(me > 0, queries[0:16, :].astype(F32), 0.0)
+    below = jnp.where(me < n - 1, queries[pl.ds(16 + pool_rows, 16), :].astype(F32), 0.0)
+    spread_rows(jnp.concatenate([above, below], axis=0), [(15, 0), (16, pool_rows + 1)])
+    combine(0)
+    combine(pool_rows - 1)
+    for copy in copies[:-2]:
         copy.wait()
     put_trunk.wait()
 
 
 def pair_kernel_body(
-    n, block, keys, queries, weight, trunk_in, pair_out, trunk_out, keys3, qrows, qcols, trunk_v, sem
+    n, block, keys, queries, weff, trunk_in, pair_out, trunk_out, keys3, qrows, trunk_v, sem
 ):
     step = pl.program_id(0)
     steps = pl.num_programs(0)
     width = keys.shape[0]
     pool_rows = width // n
-    me = lax.axis_index("seq")
 
     @pl.when(step == 0)
     def _():
@@ -304,35 +332,13 @@
         keys3[:, 0:128] = jnp.concatenate([zero, floats[:-1]], axis=0).astype(BF16)
         keys3[:, 128:256] = keys[...]
         keys3[:, 256:384] = jnp.concatenate([floats[1:], zero], axis=0).astype(BF16)
-        rows = queries[...].astype(F32)
-        above = jnp.where(me > 0, rows[15:16], 0.0)
-        below = jnp.where(me < n - 1, rows[16 + pool_rows : 17 + pool_rows], 0.0)
-        rows = jnp.concatenate(
-            [above, rows[16 : 16 + pool_rows], below, jnp.zeros((126 - pool_rows, 128), F32)],
-            axis=0,
-        )
-        qrows[...] = rows[0 : qrows.shape[0]]
-        cols = rows.T
-        for i in range(pool_rows + 2):
-            qcols[i] = jnp.broadcast_to(cols[:, i : i + 1], (128, 128)).astype(BF16)
+        qrows[...] = queries[pl.ds(16, pool_rows), :].astype(F32)
 
     for half in range(block // 2):
         base = step * block + half * 2
-        kernels = []
+        conv = jnp.dot(keys3[...], weff[half], preferred_element_type=F32).astype(BF16)
         for k in range(2):
-            parts = []
-            for b in range(3):
-                parts.append(
-                    qcols[base + k] * weight[0, b]
-                    + qcols[base + k + 1] * weight[1, b]
-                    + qcols[base + k + 2] * weight[2, b]
-                )
-            kernels.append(jnp.concatenate(parts, axis=0))
-        conv = jnp.dot(
-            keys3[...], jnp.concatenate(kernels, axis=1), preferred_element_type=F32
-        ).astype(BF16)
-        for k in range(2):
-            row = jnp.broadcast_to(qrows[pl.ds(base + k + 1, 1), :], (16, 128)).astype(BF16)
+            row = jnp.broadcast_to(qrows[pl.ds(base + k, 1), :], (16, 128)).astype(BF16)
             pair = (keys[...].reshape(width // 16, 16, 128) * row[None]).reshape(width, 128)
             pair_out[half * 2 + k] = pair + gelu(conv[:, k * 128 : k * 128 + 128])
 
@@ -356,15 +362,16 @@
     width = pool_rows * n
     hbm_spec = pl.BlockSpec(memory_space=pltpu.HBM)
     vmem_spec = pl.BlockSpec(memory_space=pltpu.VMEM)
-    trunk, keys, queries = pl.pallas_call(
+    trunk, keys, queries, weff = pl.pallas_call(
         functools.partial(trunk_kernel, n),
         out_shape=(
             jax.ShapeDtypeStruct((slab, channels), BF16),
             jax.ShapeDtypeStruct((width, 128), BF16),
             jax.ShapeDtypeStruct((pool_rows + 32, 128), BF16),
+            jax.ShapeDtypeStruct((pool_rows // 2, 384, 256), BF16),
         ),
-        in_specs=[hbm_spec] * 7,
-        out_specs=(hbm_spec, vmem_spec, vmem_spec),
+        in_specs=[hbm_spec] * 8,
+        out_specs=(hbm_spec, vmem_spec, vmem_spec, vmem_spec),
         scratch_shapes=[
             pltpu.VMEM((full, bases.shape[1]), jnp.int32),
             pltpu.VMEM(embed_table.shape, BF16),
@@ -373,12 +380,14 @@
             pltpu.VMEM(point_weight.shape, BF16),
             pltpu.VMEM(query_weight.shape, BF16),
             pltpu.VMEM(key_weight.shape, BF16),
+            pltpu.VMEM(pair_kernel.shape, BF16),
+            pltpu.VMEM((pool_rows + 2, 128, 128), BF16),
             pltpu.VMEM((full, embed_table.shape[0]), BF16),
             pltpu.VMEM((full, channels), F32),
             pltpu.VMEM((2, full, channels), BF16),
             pltpu.VMEM((2, full, channels), BF16),
             pltpu.VMEM((slab, channels), BF16),
-            pltpu.SemaphoreType.DMA((10,)),
+            pltpu.SemaphoreType.DMA((11,)),
             pltpu.SemaphoreType.DMA((2,)),
             pltpu.SemaphoreType.DMA((2,)),
             pltpu.SemaphoreType.DMA((2,)),
@@ -387,12 +396,26 @@
             pltpu.SemaphoreType.DMA((n - 1,)),
         ],
         compiler_params=pltpu.CompilerParams(
-            collective_id=0, has_side_effects=True, vmem_limit_bytes=63 * 1024 * 1024
+            collective_id=0, has_side_effects=True, vmem_limit_bytes=32 * 1024 * 1024
         ),
         name="trunk_and_gather",
-    )(bases, embed_table, norm_gains, depth_taps.swapaxes(0, 1), point_weight, query_weight, key_weight)
-
-    block = 4
+    )(
+        *(
+            pltpu.with_memory_space_constraint(array, pltpu.HBM)
+            for array in (
+                bases,
+                embed_table,
+                norm_gains,
+                depth_taps.swapaxes(0, 1),
+                point_weight,
+                query_weight,
+                key_weight,
+                pair_kernel,
+            )
+        )
+    )
+
+    block = 8
     pair_map, trunk = pl.pallas_call(
         functools.partial(pair_kernel_body, n, block),
         grid=(pool_rows // block,),
@@ -403,20 +426,19 @@
         in_specs=[
             pl.BlockSpec((width, 128), lambda i: (0, 0)),
             pl.BlockSpec((pool_rows + 32, 128), lambda i: (0, 0)),
-            pl.BlockSpec((3, 3, 128, 128), lambda i: (0, 0, 0, 0)),
+            pl.BlockSpec((block // 2, 384, 256), lambda i: (i, 0, 0)),
             hbm_spec,
         ],
         out_specs=(pl.BlockSpec((block, width, 128), lambda i: (i, 0, 0)), hbm_spec),
         scratch_shapes=[
             pltpu.VMEM((width, 384), BF16),
-            pltpu.VMEM((pool_rows + 8, 128), F32),
-            pltpu.VMEM((pool_rows + 2, 128, 128), BF16),
+            pltpu.VMEM((pool_rows, 128), F32),
             pltpu.VMEM((slab, channels), BF16),
             pltpu.SemaphoreType.DMA((2,)),
         ],
-        compiler_params=pltpu.CompilerParams(vmem_limit_bytes=63 * 1024 * 1024),
+        compiler_params=pltpu.CompilerParams(vmem_limit_bytes=32 * 1024 * 1024),
         name="pair_map",
-    )(keys, queries, pair_kernel, trunk)
+    )(keys, queries, weff, trunk)
     return (trunk, pair_map)
 
 

time: 32.7 us -> 29.2 us (0.89)
  Pallas kernels: 31.9 us -> 28.4 us
    pallas_call x1, Pallas kernels: 8.48 us -> 5.24 us  [on_device(): pl.pallas_call(functools.partial(pair_kernel_body, n, block), grid=(pool_...]
where the time goes in v4:
time: 29.2 us; the launch traced here: 29 us
  Pallas kernels  28.4 us (97%)
  between operations  0.64 us (2%)
    pallas_call x1, Pallas kernels, on_device(): pl.pallas_call(functools.partial(trunk_kernel, n), out_shape=(jax.ShapeDt...  23.2 us
    pallas_call x1, Pallas kernels, on_device(): pl.pallas_call(functools.partial(pair_kernel_body, n, block), grid=(pool_...  5.24 us

profile of v4, /device:TPU:0, one launch (start us, length us, event | category | flops | bytes accessed | tf_op | source)
XLA Modules:
  0.0 29.0 jit_solution(5826016244565254778)
XLA Ops:
  0.6 23.2 %trunk_and_gather.1 = (bf16[512,768]{1,0:T(8,128)(2,1)S(1)}, bf16[512,128]{1,0:T(8,128)(2,1)S(1)}, bf16[64,128]{1,0:T(8,128)(2,1)S(1)}, bf16[16,384,256]{2,1,0:T(8,128)(2,1)S(1)}) custom-call(s32[512,128]{1,0:T(8,128)} %bases.1, bf16[512,768]{1,0:T(8,128)(2,1)} %table.1, f32[3,768]{1,0:T(4,128)} %gains.1, f32[5,3,768]{2,1,0:T(4,128)} %bitcast.1, ...), custom_call_target="tpu_custom_call" | custom-call | tf_op jit(solution)/shard_map/trunk_and_gather/pallas_call | solution.py:365
  23.8 5.2 %pair_map.1 = (bf16[32,512,128]{2,1,0:T(8,128)(2,1)}, bf16[512,768]{1,0:T(8,128)(2,1)}) custom-call(bf16[512,128]{1,0:T(8,128)(2,1)S(1)} %get-tuple-element.8.keys, bf16[64,128]{1,0:T(8,128)(2,1)S(1)} %get-tuple-element.9.queries, bf16[16,384,256]{2,1,0:T(8,128)(2,1)S(1)} %get-tuple-element.10.weff, bf16[512,768]{1,0:T(8,128)(2,1)S(1)} %get-tuple-element.11.trunk_in), custom_call_target="tpu_custom_call" | custom-call | tf_op jit(solution)/shard_map/pair_map/pallas_call | solution.py:419

commit v5 on v4

--- a/solution.py
+++ b/solution.py
@@ -19,15 +19,8 @@
 BF16 = jnp.bfloat16
 
 
-def gelu(v):
-    half = 0.5 * v
-    return half + half * jnp.tanh(v * (GELU_A + GELU_B * (v * v)))
-
-
-def blocks_of(rows):
-    units = rows // 16
-    sizes = [(units + 2 - k) // 3 * 16 for k in range(3)]
-    return [(sum(sizes[:k]), sizes[k]) for k in range(3)]
+def gelu_of_half(half):
+    return half + half * jnp.tanh(half * (2 * GELU_A + 8 * GELU_B * (half * half)))
 
 
 def pieces_of(low, rows, most):
@@ -157,6 +150,12 @@
     reaches = [2 * s for s in DILATIONS]
     lows = [HALO - sum(reaches[layer + 1 :]) for layer in range(3)]
     scaled = []
+    edge = lows[0] + (full // 2 - lows[0]) // 16 * 16 + 32
+    blocks = []
+    for layer in range(3):
+        if layer > 0:
+            edge -= reaches[layer]
+        blocks.append(((lows[layer], edge - lows[layer]), (edge, full - lows[layer] - edge)))
 
     def norm_piece(layer, r, rows):
         floats = xs[pl.ds(r, rows), :]
@@ -188,13 +187,13 @@
                 part = nrm[layer % 2, pl.ds(at, rows), pl.ds(col, 128)]
             term = part * scaled[layer][t : t + 1, col : col + 128]
             total = term if total is None else total + term
-        act[layer % 2, pl.ds(r, rows), pl.ds(col, 128)] = gelu(total)
+        act[layer % 2, pl.ds(r, rows), pl.ds(col, 128)] = gelu_of_half(total)
 
     def convs(layer, k):
-        at, size = blocks_of(full - 2 * lows[layer])[k]
+        at, size = blocks[layer][k]
         return [
             functools.partial(conv_piece, layer, r, rows, col)
-            for r, rows in pieces_of(lows[layer] + at, size, 112)
+            for r, rows in pieces_of(at, size, 112)
             for col in range(0, channels, 128)
         ]
 
@@ -210,17 +209,16 @@
             trunk_v[pl.ds(r - HALO, rows), pl.ds(col, 256)] = mixed.astype(BF16)
 
     def mixes(layer, k):
-        at, size = blocks_of(full - 2 * lows[layer])[k]
+        at, size = blocks[layer][k]
         return [
-            functools.partial(mix_piece, layer, lows[layer] + at, size, col)
+            functools.partial(mix_piece, layer, at, size, col)
             for col in range(0, channels, 256)
         ]
 
     def next_norms(layer, k):
         if layer == 2:
             return []
-        at, size = blocks_of(full - 2 * lows[layer])[k]
-        return norms(layer + 1, lows[layer] + at, size)
+        return norms(layer + 1, *blocks[layer][k])
 
     get_table.wait()
     for at in range(0, slab, slab // 2):
@@ -235,17 +233,16 @@
     for weight in weights:
         weight.wait()
     for layer in range(3):
-        scaled.append((taps_v[:, layer] * gains_v[pl.ds(layer, 1), :]).astype(BF16))
+        scaled.append((taps_v[:, layer] * (0.5 * gains_v[pl.ds(layer, 1), :])).astype(BF16))
     for task in norms(0, 0, HALO) + norms(0, HALO + slab, HALO):
         task()
 
     interleave(convs(0, 0), [])
     for layer in range(3):
         interleave(mixes(layer, 0), convs(layer, 1))
-        interleave(mixes(layer, 1), next_norms(layer, 0) + convs(layer, 2))
         following = convs(layer + 1, 0) if layer < 2 else []
-        interleave(mixes(layer, 2), next_norms(layer, 1) + following)
-        interleave([], next_norms(layer, 2))
+        interleave(mixes(layer, 1), next_norms(layer, 0) + following)
+        interleave([], next_norms(layer, 1))
 
     put_trunk = pltpu.make_async_copy(trunk_v, trunk_out, local_sem.at[9])
     put_trunk.start()
@@ -289,7 +286,7 @@
 
     def spread_rows(rows, places):
         short = 128 - rows.shape[0]
-        cols = jnp.concatenate([rows, jnp.zeros((short, 128), F32)], axis=0).T
+        cols = (0.5 * jnp.concatenate([rows, jnp.zeros((short, 128), F32)], axis=0)).T
         for source, target in places:
             qcols[target] = jnp.broadcast_to(cols[:, source : source + 1], (128, 128)).astype(BF16)
 
@@ -340,7 +337,7 @@
         for k in range(2):
             row = jnp.broadcast_to(qrows[pl.ds(base + k, 1), :], (16, 128)).astype(BF16)
             pair = (keys[...].reshape(width // 16, 16, 128) * row[None]).reshape(width, 128)
-            pair_out[half * 2 + k] = pair + gelu(conv[:, k * 128 : k * 128 + 128])
+            pair_out[half * 2 + k] = pair + gelu_of_half(conv[:, k * 128 : k * 128 + 128])
 
     @pl.when(step == 0)
     def _():

time: 29.2 us -> 28.9 us (0.990)
  no operation moved by 1% of the time
where the time goes in v5:
time: 28.9 us; the launch traced here: 28.8 us
  Pallas kernels  28.2 us (98%)
  between operations  0.64 us (2%)
    pallas_call x1, Pallas kernels, on_device(): pl.pallas_call(functools.partial(trunk_kernel, n), out_shape=(jax.ShapeDt...  23 us
    pallas_call x1, Pallas kernels, on_device(): pl.pallas_call(functools.partial(pair_kernel_body, n, block), grid=(pool_...  5.12 us

profile of v5, /device:TPU:0, one launch (start us, length us, event | category | flops | bytes accessed | tf_op | source)
XLA Modules:
  0.0 28.8 jit_solution(10937744336913305015)
XLA Ops:
  0.6 23.0 %trunk_and_gather.1 = (bf16[512,768]{1,0:T(8,128)(2,1)S(1)}, bf16[512,128]{1,0:T(8,128)(2,1)S(1)}, bf16[64,128]{1,0:T(8,128)(2,1)S(1)}, bf16[16,384,256]{2,1,0:T(8,128)(2,1)S(1)}) custom-call(s32[512,128]{1,0:T(8,128)} %bases.1, bf16[512,768]{1,0:T(8,128)(2,1)} %table.1, f32[3,768]{1,0:T(4,128)} %gains.1, f32[5,3,768]{2,1,0:T(4,128)} %bitcast.1, ...), custom_call_target="tpu_custom_call" | custom-call | tf_op jit(solution)/shard_map/trunk_and_gather/pallas_call | solution.py:362
  23.7 5.1 %pair_map.1 = (bf16[32,512,128]{2,1,0:T(8,128)(2,1)}, bf16[512,768]{1,0:T(8,128)(2,1)}) custom-call(bf16[512,128]{1,0:T(8,128)(2,1)S(1)} %get-tuple-element.8.keys, bf16[64,128]{1,0:T(8,128)(2,1)S(1)} %get-tuple-element.9.queries, bf16[16,384,256]{2,1,0:T(8,128)(2,1)S(1)} %get-tuple-element.10.weff, bf16[512,768]{1,0:T(8,128)(2,1)S(1)} %get-tuple-element.11.trunk_in), custom_call_target="tpu_custom_call" | custom-call | tf_op jit(solution)/shard_map/pair_map/pallas_call | solution.py:416

commit v6 on v5

--- a/solution.py
+++ b/solution.py
@@ -25,17 +25,6 @@
 
 def pieces_of(low, rows, most):
     return [(low + at, min(most, rows - at)) for at in range(0, rows, most)]
-
-
-def interleave(first, second):
-    count = max(len(first), len(second), 1)
-    done = [0, 0]
-    for k in range(count):
-        for which, tasks in enumerate((first, second)):
-            target = len(tasks) * (k + 1) // count
-            while done[which] < target:
-                tasks[done[which]]()
-                done[which] += 1
 
 
 def trunk_kernel(
@@ -61,6 +50,7 @@
     kw_v,
     weight_v,
     qcols,
+    scaled,
     hot,
     xs,
     nrm,
@@ -116,7 +106,9 @@
         hot[pl.ds(start, rows), :] = jnp.where(wide == letter, 1.0, 0.0).astype(BF16)
 
     def embed(start, rows):
-        for col in range(0, channels, 256):
+        @pl.loop(0, channels // 256)
+        def _(c):
+            col = pl.multiple_of(c * 256, 256)
             xs[pl.ds(start, rows), pl.ds(col, 256)] = jnp.dot(
                 hot[pl.ds(start, rows), :],
                 table_v[:, pl.ds(col, 256)],
@@ -149,7 +141,6 @@
     last_row = n * slab
     reaches = [2 * s for s in DILATIONS]
     lows = [HALO - sum(reaches[layer + 1 :]) for layer in range(3)]
-    scaled = []
     edge = lows[0] + (full // 2 - lows[0]) // 16 * 16 + 32
     blocks = []
     for layer in range(3):
@@ -160,17 +151,21 @@
     def norm_piece(layer, r, rows):
         floats = xs[pl.ds(r, rows), :]
         mean = jnp.sum(floats * floats, axis=1, keepdims=True) * (1.0 / channels)
-        scale = lax.rsqrt(mean + 1e-6)
-        if r < HALO or r + rows > HALO + slab:
-            place = first_row + r + lax.broadcasted_iota(jnp.int32, (rows, 1), 0)
-            inside = jnp.logical_and(place >= 0, place < last_row)
-            scale = jnp.where(inside, scale, 0.0)
+        place = first_row + r + lax.broadcasted_iota(jnp.int32, (rows, 1), 0)
+        inside = jnp.logical_and(place >= 0, place < last_row)
+        scale = jnp.where(inside, lax.rsqrt(mean + 1e-6), 0.0)
         nrm[layer % 2, pl.ds(r, rows), :] = (floats * scale).astype(BF16)
 
     def norms(layer, low, rows):
-        return [
-            functools.partial(norm_piece, layer, r, size) for r, size in pieces_of(low, rows, 32)
-        ]
+        whole = rows // 64
+
+        @pl.loop(0, whole)
+        def _(k):
+            for part in range(4):
+                norm_piece(layer, pl.multiple_of(low + k * 64 + part * 16, 16), 16)
+
+        for at in range(whole * 64, rows, 16):
+            norm_piece(layer, pl.multiple_of(low + at, 16), 16)
 
     def conv_piece(layer, r, rows, col):
         s = DILATIONS[layer]
@@ -185,19 +180,19 @@
                 part = near[at - low : at - low + rows]
             else:
                 part = nrm[layer % 2, pl.ds(at, rows), pl.ds(col, 128)]
-            term = part * scaled[layer][t : t + 1, col : col + 128]
+            tap = scaled[layer, t, :, pl.ds(col, 128)]
+            term = part.reshape(rows // 16, 16, 128) * tap[None]
             total = term if total is None else total + term
-        act[layer % 2, pl.ds(r, rows), pl.ds(col, 128)] = gelu_of_half(total)
-
-    def convs(layer, k):
-        at, size = blocks[layer][k]
-        return [
-            functools.partial(conv_piece, layer, r, rows, col)
-            for r, rows in pieces_of(at, size, 112)
-            for col in range(0, channels, 128)
-        ]
-
-    def mix_piece(layer, r, rows, col):
+        act[layer % 2, pl.ds(r, rows), pl.ds(col, 128)] = gelu_of_half(total).reshape(rows, 128)
+
+    def conv_chunk(layer, k, chunk):
+        for half in range(2):
+            for r, rows in pieces_of(*blocks[layer][k], 112):
+                conv_piece(layer, r, rows, pl.multiple_of(chunk * 256 + half * 128, 128))
+
+    def mix_chunk(layer, k, chunk):
+        r, rows = blocks[layer][k]
+        col = pl.multiple_of(chunk * 256, 256)
         mixed = xs[pl.ds(r, rows), pl.ds(col, 256)] + jnp.dot(
             act[layer % 2, pl.ds(r, rows), :],
             point_v[layer, :, pl.ds(col, 256)],
@@ -208,41 +203,48 @@
         else:
             trunk_v[pl.ds(r - HALO, rows), pl.ds(col, 256)] = mixed.astype(BF16)
 
-    def mixes(layer, k):
-        at, size = blocks[layer][k]
-        return [
-            functools.partial(mix_piece, layer, at, size, col)
-            for col in range(0, channels, 256)
-        ]
-
-    def next_norms(layer, k):
-        if layer == 2:
-            return []
-        return norms(layer + 1, *blocks[layer][k])
-
     get_table.wait()
-    for at in range(0, slab, slab // 2):
-        embed(HALO + at, slab // 2)
-    for task in norms(0, HALO, slab):
-        task()
+    embed(HALO, slab)
+    norms(0, HALO, slab)
     to_right.wait()
     to_left.wait()
-    for start in (0, HALO + slab):
+
+    @pl.loop(0, 2)
+    def _(side):
+        start = pl.multiple_of(side * (HALO + slab), 16)
         one_hot(start, HALO)
         embed(start, HALO)
-    for weight in weights:
-        weight.wait()
+        norms(0, start, HALO)
+
+    for weight_copy in weights:
+        weight_copy.wait()
     for layer in range(3):
-        scaled.append((taps_v[:, layer] * (0.5 * gains_v[pl.ds(layer, 1), :])).astype(BF16))
-    for task in norms(0, 0, HALO) + norms(0, HALO + slab, HALO):
-        task()
-
-    interleave(convs(0, 0), [])
+        for t in range(KW):
+            row = taps_v[pl.ds(t, 1), layer, :] * (0.5 * gains_v[pl.ds(layer, 1), :])
+            scaled[layer, t] = jnp.broadcast_to(row, (16, channels)).astype(BF16)
+
+    @pl.loop(0, channels // 256)
+    def _(chunk):
+        conv_chunk(0, 0, chunk)
+
     for layer in range(3):
-        interleave(mixes(layer, 0), convs(layer, 1))
-        following = convs(layer + 1, 0) if layer < 2 else []
-        interleave(mixes(layer, 1), next_norms(layer, 0) + following)
-        interleave([], next_norms(layer, 1))
+
+        @pl.loop(0, channels // 256)
+        def _(chunk, layer=layer):
+            mix_chunk(layer, 0, chunk)
+            conv_chunk(layer, 1, chunk)
+
+        if layer < 2:
+            norms(layer + 1, *blocks[layer][0])
+
+        @pl.loop(0, channels // 256)
+        def _(chunk, layer=layer):
+            mix_chunk(layer, 1, chunk)
+            if layer < 2:
+                conv_chunk(layer + 1, 0, chunk)
+
+        if layer < 2:
+            norms(layer + 1, *blocks[layer][1])
 
     put_trunk = pltpu.make_async_copy(trunk_v, trunk_out, local_sem.at[9])
     put_trunk.start()
@@ -290,24 +292,32 @@
         for source, target in places:
             qcols[target] = jnp.broadcast_to(cols[:, source : source + 1], (128, 128)).astype(BF16)
 
-    def combine(i):
-        for b in range(3):
-            weff[i // 2, pl.ds(b * 128, 128), pl.ds(i % 2 * 128, 128)] = (
-                qcols[i] * weight_v[0, b]
-                + qcols[i + 1] * weight_v[1, b]
-                + qcols[i + 2] * weight_v[2, b]
-            )
+    def combine(pair):
+        for k in range(2):
+            i = pair * 2 + k
+            for b in range(3):
+                weff[pair, pl.ds(b * 128, 128), pl.ds(k * 128, 128)] = (
+                    qcols[i] * weight_v[0, b]
+                    + qcols[i + 1] * weight_v[1, b]
+                    + qcols[i + 2] * weight_v[2, b]
+                )
 
     spread_rows(own_queries.astype(F32), [(i, i + 1) for i in range(pool_rows)])
-    for i in range(1, pool_rows - 1):
-        combine(i)
+
+    @pl.loop(1, pool_rows // 2 - 1)
+    def _(pair):
+        combine(pair)
+
     for copy in copies[-2:]:
         copy.wait()
     above = jnp.where(me > 0, queries[0:16, :].astype(F32), 0.0)
     below = jnp.where(me < n - 1, queries[pl.ds(16 + pool_rows, 16), :].astype(F32), 0.0)
     spread_rows(jnp.concatenate([above, below], axis=0), [(15, 0), (16, pool_rows + 1)])
-    combine(0)
-    combine(pool_rows - 1)
+
+    @pl.loop(0, 2)
+    def _(end):
+        combine(end * (pool_rows // 2 - 1))
+
     for copy in copies[:-2]:
         copy.wait()
     put_trunk.wait()
@@ -379,6 +389,7 @@
             pltpu.VMEM(key_weight.shape, BF16),
             pltpu.VMEM(pair_kernel.shape, BF16),
             pltpu.VMEM((pool_rows + 2, 128, 128), BF16),
+            pltpu.VMEM((3, KW, 16, channels), BF16),
             pltpu.VMEM((full, embed_table.shape[0]), BF16),
             pltpu.VMEM((full, channels), F32),
             pltpu.VMEM((2, full, channels), BF16),

time: 28.9 us -> 33.8 us (1.17)
  Pallas kernels: 28.2 us -> 33 us
    pallas_call x1, Pallas kernels: 23 us -> 27.9 us  [on_device(): pl.pallas_call(functools.partial(trunk_kernel, n), out_shape=(jax.ShapeDt...]
where the time goes in v6:
time: 33.8 us; the launch traced here: 33.6 us
  Pallas kernels  33 us (98%)
  between operations  0.64 us (2%)
    pallas_call x1, Pallas kernels, on_device(): pl.pallas_call(functools.partial(trunk_kernel, n), out_shape=(jax.ShapeDt...  27.9 us
    pallas_call x1, Pallas kernels, on_device(): pl.pallas_call(functools.partial(pair_kernel_body, n, block), grid=(pool_...  5.11 us

profile of v6, /device:TPU:0, one launch (start us, length us, event | category | flops | bytes accessed | tf_op | source)
XLA Modules:
  0.0 33.6 jit_solution(12267387362163899859)
XLA Ops:
  0.6 27.9 %trunk_and_gather.1 = (bf16[512,768]{1,0:T(8,128)(2,1)S(1)}, bf16[512,128]{1,0:T(8,128)(2,1)S(1)}, bf16[64,128]{1,0:T(8,128)(2,1)S(1)}, bf16[16,384,256]{2,1,0:T(8,128)(2,1)S(1)}) custom-call(s32[512,128]{1,0:T(8,128)} %bases.1, bf16[512,768]{1,0:T(8,128)(2,1)} %table.1, f32[3,768]{1,0:T(4,128)} %gains.1, f32[5,3,768]{2,1,0:T(4,128)} %bitcast.1, ...), custom_call_target="tpu_custom_call" | custom-call | tf_op jit(solution)/shard_map/trunk_and_gather/pallas_call | solution.py:372
  28.5 5.1 %pair_map.1 = (bf16[32,512,128]{2,1,0:T(8,128)(2,1)}, bf16[512,768]{1,0:T(8,128)(2,1)}) custom-call(bf16[512,128]{1,0:T(8,128)(2,1)S(1)} %get-tuple-element.8.keys, bf16[64,128]{1,0:T(8,128)(2,1)S(1)} %get-tuple-element.9.queries, bf16[16,384,256]{2,1,0:T(8,128)(2,1)S(1)} %get-tuple-element.10.weff, bf16[512,768]{1,0:T(8,128)(2,1)S(1)} %get-tuple-element.11.trunk_in), custom_call_target="tpu_custom_call" | custom-call | tf_op jit(solution)/shard_map/pair_map/pallas_call | solution.py:427

commit v7 on v5

--- a/solution.py
+++ b/solution.py
@@ -93,7 +93,7 @@
         copy.start()
         return copy
 
-    own = fetch(bases, base_v.at[pl.ds(HALO, slab)], 0)
+    own = fetch(bases, base_v.at[pl.ds(2 * HALO, slab)], 0)
     get_table = fetch(table, table_v, 1)
     weights = [fetch(gains, gains_v, 2), fetch(taps, taps_v, 3)]
     for layer in range(3):
@@ -115,16 +115,18 @@
         wide = jnp.dot(codes, spread, preferred_element_type=F32)
         hot[pl.ds(start, rows), :] = jnp.where(wide == letter, 1.0, 0.0).astype(BF16)
 
-    def embed(start, rows):
+    def embed(start, rows, places):
         for col in range(0, channels, 256):
-            xs[pl.ds(start, rows), pl.ds(col, 256)] = jnp.dot(
+            embedded = jnp.dot(
                 hot[pl.ds(start, rows), :],
                 table_v[:, pl.ds(col, 256)],
                 preferred_element_type=F32,
             )
+            for source, target, count in places:
+                xs[pl.ds(target, count), pl.ds(col, 256)] = embedded[source : source + count]
 
     own.wait()
-    one_hot(HALO, slab)
+    one_hot(2 * HALO, slab)
     pl.semaphore_wait(barrier, n - 1)
     to_right = pltpu.make_async_remote_copy(
         src_ref=bases.at[pl.ds(slab - HALO, HALO)],
@@ -137,7 +139,7 @@
     to_right.start()
     to_left = pltpu.make_async_remote_copy(
         src_ref=bases.at[pl.ds(0, HALO)],
-        dst_ref=base_v.at[pl.ds(HALO + slab, HALO)],
+        dst_ref=base_v.at[pl.ds(HALO, HALO)],
         send_sem=halo_send.at[1],
         recv_sem=halo_recv.at[1],
         device_id={"seq": left},
@@ -222,14 +224,13 @@
 
     get_table.wait()
     for at in range(0, slab, slab // 2):
-        embed(HALO + at, slab // 2)
+        embed(2 * HALO + at, slab // 2, [(0, HALO + at, slab // 2)])
     for task in norms(0, HALO, slab):
         task()
     to_right.wait()
     to_left.wait()
-    for start in (0, HALO + slab):
-        one_hot(start, HALO)
-        embed(start, HALO)
+    one_hot(0, 2 * HALO)
+    embed(0, 2 * HALO, [(0, 0, HALO), (HALO, HALO + slab, HALO)])
     for weight in weights:
         weight.wait()
     for layer in range(3):
@@ -313,40 +314,43 @@
     put_trunk.wait()
 
 
-def pair_kernel_body(
-    n, block, keys, queries, weff, trunk_in, pair_out, trunk_out, keys3, qrows, trunk_v, sem
-):
-    step = pl.program_id(0)
-    steps = pl.num_programs(0)
+def pair_kernel_body(n, keys, queries, weff, trunk_in, pair_out, trunk_out, keys3, made, sem):
     width = keys.shape[0]
     pool_rows = width // n
-
-    @pl.when(step == 0)
-    def _():
-        pltpu.make_async_copy(trunk_in, trunk_v, sem.at[0]).start()
-        floats = keys[...].astype(F32)
-        zero = jnp.zeros((1, 128), F32)
-        keys3[:, 0:128] = jnp.concatenate([zero, floats[:-1]], axis=0).astype(BF16)
-        keys3[:, 128:256] = keys[...]
-        keys3[:, 256:384] = jnp.concatenate([floats[1:], zero], axis=0).astype(BF16)
-        qrows[...] = queries[pl.ds(16, pool_rows), :].astype(F32)
-
-    for half in range(block // 2):
-        base = step * block + half * 2
-        conv = jnp.dot(keys3[...], weff[half], preferred_element_type=F32).astype(BF16)
+    pairs = pool_rows // 2
+
+    put_trunk = pltpu.make_async_copy(trunk_in, trunk_out, sem.at[pairs])
+    put_trunk.start()
+    floats = keys[...].astype(F32)
+    zero = jnp.zeros((1, 128), F32)
+    keys3[:, 0:128] = jnp.concatenate([zero, floats[:-1]], axis=0).astype(BF16)
+    keys3[:, 128:256] = keys[...]
+    keys3[:, 256:384] = jnp.concatenate([floats[1:], zero], axis=0).astype(BF16)
+    rows = queries[pl.ds(16, pool_rows), :].astype(F32)
+
+    def convolve(i):
+        return jnp.dot(keys3[...], weff[i], preferred_element_type=F32).astype(BF16)
+
+    copies = []
+    following = convolve(0)
+    for i in range(pairs):
+        conv = following
+        if i + 1 < pairs:
+            following = convolve(i + 1)
         for k in range(2):
-            row = jnp.broadcast_to(qrows[pl.ds(base + k, 1), :], (16, 128)).astype(BF16)
+            at = i * 2 + k
+            row = jnp.broadcast_to(rows[at : at + 1], (16, 128)).astype(BF16)
             pair = (keys[...].reshape(width // 16, 16, 128) * row[None]).reshape(width, 128)
-            pair_out[half * 2 + k] = pair + gelu_of_half(conv[:, k * 128 : k * 128 + 128])
-
-    @pl.when(step == 0)
-    def _():
-        pltpu.make_async_copy(trunk_in, trunk_v, sem.at[0]).wait()
-        pltpu.make_async_copy(trunk_v, trunk_out, sem.at[1]).start()
-
-    @pl.when(step == steps - 1)
-    def _():
-        pltpu.make_async_copy(trunk_v, trunk_out, sem.at[1]).wait()
+            made[at] = pair + gelu_of_half(conv[:, k * 128 : k * 128 + 128])
+        copies.append(
+            pltpu.make_async_copy(
+                made.at[pl.ds(i * 2, 2)], pair_out.at[pl.ds(i * 2, 2)], sem.at[i]
+            )
+        )
+        copies[-1].start()
+    for copy in copies:
+        copy.wait()
+    put_trunk.wait()
 
 
 def on_device(
@@ -412,26 +416,18 @@
         )
     )
 
-    block = 8
     pair_map, trunk = pl.pallas_call(
-        functools.partial(pair_kernel_body, n, block),
-        grid=(pool_rows // block,),
+        functools.partial(pair_kernel_body, n),
         out_shape=(
             jax.ShapeDtypeStruct((pool_rows, width, 128), BF16),
             jax.ShapeDtypeStruct((slab, channels), BF16),
         ),
-        in_specs=[
-            pl.BlockSpec((width, 128), lambda i: (0, 0)),
-            pl.BlockSpec((pool_rows + 32, 128), lambda i: (0, 0)),
-            pl.BlockSpec((block // 2, 384, 256), lambda i: (i, 0, 0)),
-            hbm_spec,
-        ],
-        out_specs=(pl.BlockSpec((block, width, 128), lambda i: (i, 0, 0)), hbm_spec),
+        in_specs=[vmem_spec] * 4,
+        out_specs=(hbm_spec, hbm_spec),
         scratch_shapes=[
             pltpu.VMEM((width, 384), BF16),
-            pltpu.VMEM((pool_rows, 128), F32),
-            pltpu.VMEM((slab, channels), BF16),
-            pltpu.SemaphoreType.DMA((2,)),
+            pltpu.VMEM((pool_rows, width, 128), BF16),
+            pltpu.SemaphoreType.DMA((pool_rows // 2 + 1,)),
         ],
         compiler_params=pltpu.CompilerParams(vmem_limit_bytes=32 * 1024 * 1024),
         name="pair_map",

time: 28.9 us -> 28.1 us (0.972)
  Pallas kernels: 28.2 us -> 27.2 us
    pallas_call x1, Pallas kernels: 5.12 us -> 4.08 us  [on_device(): pl.pallas_call(functools.partial(pair_kernel_body, n), out_shape=(jax.Sha...]
where the time goes in v7:
time: 28.1 us; the launch traced here: 28 us
  Pallas kernels  27.2 us (97%)
  between operations  0.8 us (3%)
    pallas_call x1, Pallas kernels, on_device(): pl.pallas_call(functools.partial(trunk_kernel, n), out_shape=(jax.ShapeDt...  23.1 us
    pallas_call x1, Pallas kernels, on_device(): pl.pallas_call(functools.partial(pair_kernel_body, n), out_shape=(jax.Sha...  4.08 us

profile of v7, /device:TPU:0, one launch (start us, length us, event | category | flops | bytes accessed | tf_op | source)
XLA Modules:
  0.0 28.0 jit_solution(3726521873102548845)
XLA Ops:
  0.6 23.1 %trunk_and_gather.1 = (bf16[512,768]{1,0:T(8,128)(2,1)S(1)}, bf16[512,128]{1,0:T(8,128)(2,1)S(1)}, bf16[64,128]{1,0:T(8,128)(2,1)S(1)}, bf16[16,384,256]{2,1,0:T(8,128)(2,1)S(1)}) custom-call(s32[512,128]{1,0:T(8,128)} %bases.1, bf16[512,768]{1,0:T(8,128)(2,1)} %table.1, f32[3,768]{1,0:T(4,128)} %gains.1, f32[5,3,768]{2,1,0:T(4,128)} %bitcast.1, ...), custom_call_target="tpu_custom_call" | custom-call | tf_op jit(solution)/shard_map/trunk_and_gather/pallas_call | solution.py:366
  23.7 4.1 %pair_map.1 = (bf16[32,512,128]{2,1,0:T(8,128)(2,1)}, bf16[512,768]{1,0:T(8,128)(2,1)}) custom-call(bf16[512,128]{1,0:T(8,128)(2,1)S(1)} %get-tuple-element.8.keys, bf16[64,128]{1,0:T(8,128)(2,1)S(1)} %get-tuple-element.9.queries, bf16[16,384,256]{2,1,0:T(8,128)(2,1)S(1)} %get-tuple-element.10.weff, bf16[512,768]{1,0:T(8,128)(2,1)S(1)} %get-tuple-element.11.trunk_in), custom_call_target="tpu_custom_call" | custom-call | tf_op jit(solution)/shard_map/pair_map/pallas_call | solution.py:419

commit v8 on v7

--- a/solution.py
+++ b/solution.py
@@ -239,19 +239,27 @@
         task()
 
     interleave(convs(0, 0), [])
+    def pool_part(k):
+        at, size = blocks[2][k]
+        at -= HALO
+        members = (
+            lax.broadcasted_iota(jnp.int32, (pool_rows, size), 1) // POOL
+            == lax.broadcasted_iota(jnp.int32, (pool_rows, size), 0) - at // POOL
+        )
+        pooler = jnp.where(members, 1.0 / POOL, 0.0).astype(BF16)
+        return jnp.dot(pooler, trunk_v[pl.ds(at, size), :], preferred_element_type=F32)
+
     for layer in range(3):
         interleave(mixes(layer, 0), convs(layer, 1))
         following = convs(layer + 1, 0) if layer < 2 else []
+        if layer == 2:
+            first_pooled = pool_part(0)
         interleave(mixes(layer, 1), next_norms(layer, 0) + following)
         interleave([], next_norms(layer, 1))
 
     put_trunk = pltpu.make_async_copy(trunk_v, trunk_out, local_sem.at[9])
     put_trunk.start()
-    group = lax.broadcasted_iota(jnp.int32, (pool_rows, slab), 1) // POOL
-    pooler = jnp.where(
-        group == lax.broadcasted_iota(jnp.int32, (pool_rows, slab), 0), 1.0 / POOL, 0.0
-    ).astype(BF16)
-    pooled = jnp.dot(pooler, trunk_v[...], preferred_element_type=F32).astype(BF16)
+    pooled = (first_pooled + pool_part(1)).astype(BF16)
     mine = pl.ds(pl.multiple_of(me * pool_rows, pool_rows), pool_rows)
     keys[mine, :] = jnp.dot(pooled, kw_v[...], preferred_element_type=F32).astype(BF16)
 

time: 28.1 us -> 28.2 us (level)
  no operation moved by 1% of the time
where the time goes in v8:
time: 28.2 us; the launch traced here: 28 us
  Pallas kernels  27.2 us (96%)
  between operations  0.8 us (3%)
    pallas_call x1, Pallas kernels, on_device(): pl.pallas_call(functools.partial(trunk_kernel, n), out_shape=(jax.ShapeDt...  23.2 us
    pallas_call x1, Pallas kernels, on_device(): pl.pallas_call(functools.partial(pair_kernel_body, n), out_shape=(jax.Sha...  4.08 us

profile of v8, /device:TPU:0, one launch (start us, length us, event | category | flops | bytes accessed | tf_op | source)
XLA Modules:
  0.0 28.0 jit_solution(12128990951320878891)
XLA Ops:
  0.6 23.2 %trunk_and_gather.1 = (bf16[512,768]{1,0:T(8,128)(2,1)S(1)}, bf16[512,128]{1,0:T(8,128)(2,1)S(1)}, bf16[64,128]{1,0:T(8,128)(2,1)S(1)}, bf16[16,384,256]{2,1,0:T(8,128)(2,1)S(1)}) custom-call(s32[512,128]{1,0:T(8,128)} %bases.1, bf16[512,768]{1,0:T(8,128)(2,1)} %table.1, f32[3,768]{1,0:T(4,128)} %gains.1, f32[5,3,768]{2,1,0:T(4,128)} %bitcast.1, ...), custom_call_target="tpu_custom_call" | custom-call | tf_op jit(solution)/shard_map/trunk_and_gather/pallas_call | solution.py:374
  23.8 4.1 %pair_map.1 = (bf16[32,512,128]{2,1,0:T(8,128)(2,1)}, bf16[512,768]{1,0:T(8,128)(2,1)}) custom-call(bf16[512,128]{1,0:T(8,128)(2,1)S(1)} %get-tuple-element.8.keys, bf16[64,128]{1,0:T(8,128)(2,1)S(1)} %get-tuple-element.9.queries, bf16[16,384,256]{2,1,0:T(8,128)(2,1)S(1)} %get-tuple-element.10.weff, bf16[512,768]{1,0:T(8,128)(2,1)S(1)} %get-tuple-element.11.trunk_in), custom_call_target="tpu_custom_call" | custom-call | tf_op jit(solution)/shard_map/pair_map/pallas_call | solution.py:427
